TPU v7x, 128 devices: a whole 4x4x4 slice. The times are simulated.
128 devices in a mesh: layer: 4 (over z_lo, core), lon: 32 (over z_hi, y, x).
Axes of the slice: x: 4, y: 4, z: 4 (z_hi: 2, z_lo: 2; z = z_hi * 2 + z_lo), core: 2. Of those that a mesh axis runs over, the one named last changes fastest.
Arguments:
- frames: bfloat16 [2, 32, 1024, 128], P(None, None, 'lon'), may hold values from -6 to 6
- weights: bfloat16 [4, 9, 256, 512], P('layer'), may hold values from -0.125 to 0.125
- biases: float32 [4, 512], P('layer'), may hold values from -3 to 3
- hidden_init: bfloat16 [4, 32, 1024, 128], P('layer', None, 'lon'), may hold values from -3 to 3
- cell_init: float32 [4, 32, 1024, 128], P('layer', None, 'lon'), may hold values from -5 to 5
Outputs:
- hidden_seq: bfloat16 [4, 2, 32, 1024, 128], P('layer', None, None, 'lon')
- cell_final: float32 [4, 32, 1024, 128], P('layer', None, 'lon')
All inputs are finite; a program needn't handle non-finite values.
Results may differ from a plain program's by a relative error of at most 0.0017.
Values may be sent and summed in bfloat16 or wider, within the bound.
A program may use at most 64 MiB of HBM per device.

v0:
```python
import jax
import jax.numpy as jnp
from jax import lax
from jax.sharding import PartitionSpec as P


def passed_along(value, axis, by):
    peers = lax.axis_size(axis)
    pairs = [(i, i + by) for i in range(peers) if 0 <= i + by < peers]
    return lax.ppermute(value, axis, pairs)


def extended(cells, sides, width):
    for axis, dim in sides:
        count = lax.axis_size(axis)
        head = lax.slice_in_dim(cells, 0, width, axis=dim)
        tail = lax.slice_in_dim(cells, cells.shape[dim] - width, cells.shape[dim], axis=dim)
        cells = jnp.concatenate(
            [
                lax.ppermute(tail, axis, [(i, (i + 1) % count) for i in range(count)]),
                cells,
                lax.ppermute(head, axis, [((i + 1) % count, i) for i in range(count)]),
            ],
            axis=dim,
        )
    return cells


def convolve(padded, weight, gate_bias, band_rows, band_cols):
    summed = jnp.zeros((band_rows * band_cols, weight.shape[2]), jnp.float32)
    for offset in range(9):
        row_off, col_off = (offset // 3, offset % 3)
        window_block = padded[row_off : row_off + band_rows, col_off : col_off + band_cols].reshape(
            band_rows * band_cols, -1
        )
        summed = summed + jnp.dot(window_block, weight[offset], preferred_element_type=jnp.float32)
    return summed + gate_bias[None, :]


def gate_update(gate_sums, memory):
    chans = memory.shape[-1]
    flat_memory = memory.reshape(-1, chans)
    ingate = jax.nn.sigmoid(gate_sums[:, :chans])
    forget = jax.nn.sigmoid(gate_sums[:, chans : 2 * chans])
    candidate = jnp.tanh(gate_sums[:, 2 * chans : 3 * chans])
    outgate = jax.nn.sigmoid(gate_sums[:, 3 * chans :])
    new_memory = forget * flat_memory + ingate * candidate
    new_hidden = (outgate * jnp.tanh(new_memory)).astype(jnp.bfloat16)
    return (new_hidden.reshape(memory.shape), new_memory.reshape(memory.shape))


def advance(widened, weight, gate_bias, hidden, memory, record, active, clamped):
    band_rows, band_cols = (hidden.shape[0], hidden.shape[1])

    def compute(operands):
        old_hidden, old_memory, old_record = operands
        padded = jnp.pad(widened, ((1, 1), (0, 0), (0, 0)))
        gate_sums = convolve(padded, weight, gate_bias, band_rows, band_cols)
        new_hidden, new_memory = gate_update(gate_sums, old_memory)
        new_record = lax.dynamic_update_index_in_dim(old_record, new_hidden, clamped, 0)
        return (new_hidden, new_memory, new_record)

    def keep_all(operands):
        return operands

    return lax.cond(active, compute, keep_all, (hidden, memory, record))


def local(frames, weights, biases, hidden_init, cell_init):
    layers = lax.axis_size("layer")
    section_index = lax.axis_index("layer")
    frame_count = frames.shape[0]
    weight = weights[0]
    gate_bias = biases[0]
    hidden = hidden_init[0]
    memory = cell_init[0]
    record = jnp.zeros((frame_count,) + hidden.shape, jnp.bfloat16)
    clocks = frame_count + layers - 1
    latest = jnp.zeros_like(hidden)
    for clock in range(clocks):
        arrived = passed_along(latest, "layer", 1)
        moment = clock - section_index
        active = (moment >= 0) & (moment < frame_count)
        clamped = jnp.clip(moment, 0, frame_count - 1)
        own_frame = lax.dynamic_index_in_dim(frames, clamped, 0, keepdims=False)
        source = jnp.where(section_index == 0, own_frame, arrived)
        stacked = jnp.concatenate([source, hidden], axis=-1)
        widened = extended(stacked, (("lon", 1),), 1)
        hidden, memory, record = advance(
            widened, weight, gate_bias, hidden, memory, record, active, clamped
        )
        latest = hidden
    return (record[None], memory[None])


def solution(mesh):
    in_specs = (
        P(None, None, "lon", None),
        P("layer", None, None, None),
        P("layer", None),
        P("layer", None, "lon", None),
        P("layer", None, "lon", None),
    )
    out_specs = (P("layer", None, None, "lon", None), P("layer", None, "lon", None))
    return jax.shard_map(local, mesh=mesh, in_specs=in_specs, out_specs=out_specs, check_vma=False)
```

profile of v0, /device:TPU:63, one launch (start us, length us, event | category | flops | bytes accessed | tf_op | source)
XLA Modules:
  0.0 138.2 jit_solution(12791108426503400940)
XLA Ops:
  0.6 1.7 %copy.54 = bf16[1,32,32,128]{3,2,1,0:T(8,128)(2,1)} copy(bf16[1,32,32,128]{3,2,1,0:T(8,128)(2,1)} %param.18) | data formatting | bytes 524288
  3.4 1.4 %collective-permute-start = (bf16[32,32,128]{2,1,0:T(8,128)(2,1)S(1)}, bf16[32,32,128]{2,1,0:T(8,128)(2,1)S(1)}, u32[]{:S(2)}, u32[]{:S(2)}) collective-permute-start(bf16[32,32,128]{2,1,0:T(8,128)(2,1)S(1)} %broadcast_in_dim.39), channel_id=1, source_target_pairs={{0,32},{32,64},{64,96},{1,33},{33,65},{65,97},{2,34},{34,66},{66,9... | collective-permute-start | bytes 786440 | tf_op jit(solution)/shard_map/ppermute | solution.py:10
  4.8 2.3 %collective-permute-done = bf16[32,32,128]{2,1,0:T(8,128)(2,1)S(1)} collective-permute-done((bf16[32,32,128]{2,1,0:T(8,128)(2,1)S(1)}, bf16[32,32,128]{2,1,0:T(8,128)(2,1)S(1)}, u32[]{:S(2)}, u32[]{:S(2)}) %collective-permute-start) | collective-permute-done | bytes 262176 | tf_op jit(solution)/shard_map/ppermute | solution.py:10
  9.0 2.3 %collective-permute-start.1 = (bf16[32,1,256]{2,1,0:T(2,128)(2,1)S(1)}, bf16[32,1,256]{2,1,0:T(2,128)(2,1)S(1)}, u32[]{:S(2)}, u32[]{:S(2)}) collective-permute-start(bf16[32,1,256]{2,1,0:T(2,128)(2,1)S(1)} %get-tuple-element.214), channel_id=1, source_target_pairs={{0,1},{1,2},{2,3},{3,4},{4,5},{5,6},{6,7},{7,8},{8,9},{9,10},{10,1... | collective-permute-start | bytes 49160 | tf_op jit(solution)/shard_map/ppermute | solution.py:20
  12.4 7.5 %collective-permute-done.2 = bf16[32,1,256]{2,1,0:T(2,128)(2,1)S(1)} collective-permute-done((bf16[32,1,256]{2,1,0:T(2,128)(2,1)S(1)}, bf16[32,1,256]{2,1,0:T(2,128)(2,1)S(1)}, u32[]{:S(2)}, u32[]{:S(2)}) %collective-permute-start.2) | collective-permute-done | bytes 16416 | tf_op jit(solution)/shard_map/ppermute | solution.py:22
  23.4 8.2 %collective-permute-done.3 = bf16[32,32,128]{2,1,0:T(8,128)(2,1)} collective-permute-done((bf16[32,32,128]{2,1,0:T(8,128)(2,1)}, bf16[32,32,128]{2,1,0:T(8,128)(2,1)}, u32[]{:S(2)}, u32[]{:S(2)}) %collective-permute-start.3) | collective-permute-done | bytes 262176 | tf_op jit(solution)/shard_map/ppermute | solution.py:10
  34.3 1.5 %collective-permute-start.5 = (bf16[32,1,256]{2,1,0:T(2,128)(2,1)S(1)}, bf16[32,1,256]{2,1,0:T(2,128)(2,1)S(1)}, u32[]{:S(2)}, u32[]{:S(2)}) collective-permute-start(bf16[32,1,256]{2,1,0:T(2,128)(2,1)S(1)} %get-tuple-element.213), channel_id=1, source_target_pairs={{1,0},{2,1},{3,2},{4,3},{5,4},{6,5},{7,6},{8,7},{9,8},{10,9},{11,1... | collective-permute-start | bytes 49160 | tf_op jit(solution)/shard_map/ppermute | solution.py:22
  37.0 5.8 %collective-permute-done.5 = bf16[32,1,256]{2,1,0:T(2,128)(2,1)S(1)} collective-permute-done((bf16[32,1,256]{2,1,0:T(2,128)(2,1)S(1)}, bf16[32,1,256]{2,1,0:T(2,128)(2,1)S(1)}, u32[]{:S(2)}, u32[]{:S(2)}) %collective-permute-start.5) | collective-permute-done | bytes 16416 | tf_op jit(solution)/shard_map/ppermute | solution.py:22
  42.8 1.4 %pad_maximum_fusion.1 = bf16[32,34,256]{2,1,0:T(8,128)(2,1)S(1)} fusion(bf16[32,1,256]{2,1,0:T(2,128)(2,1)S(1)} %collective-permute-done.5, bf16[32,32,128]{2,1,0:T(8,128)(2,1)} %get-tuple-element.137, bf16[32,32,128]{2,1,0:T(8,128)(2,1)} %copy-done.4, bf16[32,1,256]{2,1,0:T(2,128)(2,1)S(1)} %collective-permute-done.4), kind=kLoop, calls=%fused_computation.261 | loop fusion | flops 2228224 | bytes 1114112 | tf_op jit(solution)/shard_map/concatenate | solution.py:18
  45.6 7.8 %collective-permute-done.6 = bf16[32,32,128]{2,1,0:T(8,128)(2,1)} collective-permute-done((bf16[32,32,128]{2,1,0:T(8,128)(2,1)}, bf16[32,32,128]{2,1,0:T(8,128)(2,1)}, u32[]{:S(2)}, u32[]{:S(2)}) %collective-permute-start.6) | collective-permute-done | bytes 262176 | tf_op jit(solution)/shard_map/ppermute | solution.py:10
  56.3 1.5 %collective-permute-start.8 = (bf16[32,1,256]{2,1,0:T(2,128)(2,1)S(1)}, bf16[32,1,256]{2,1,0:T(2,128)(2,1)S(1)}, u32[]{:S(2)}, u32[]{:S(2)}) collective-permute-start(bf16[32,1,256]{2,1,0:T(2,128)(2,1)S(1)} %get-tuple-element.211), channel_id=1, source_target_pairs={{1,0},{2,1},{3,2},{4,3},{5,4},{6,5},{7,6},{8,7},{9,8},{10,9},{11,1... | collective-permute-start | bytes 49160 | tf_op jit(solution)/shard_map/ppermute | solution.py:22
  59.1 5.8 %collective-permute-done.8 = bf16[32,1,256]{2,1,0:T(2,128)(2,1)S(1)} collective-permute-done((bf16[32,1,256]{2,1,0:T(2,128)(2,1)S(1)}, bf16[32,1,256]{2,1,0:T(2,128)(2,1)S(1)}, u32[]{:S(2)}, u32[]{:S(2)}) %collective-permute-start.8) | collective-permute-done | bytes 16416 | tf_op jit(solution)/shard_map/ppermute | solution.py:22
  64.9 1.4 %pad_maximum_fusion.2 = bf16[32,34,256]{2,1,0:T(8,128)(2,1)S(1)} fusion(bf16[32,1,256]{2,1,0:T(2,128)(2,1)S(1)} %collective-permute-done.8, bf16[32,32,128]{2,1,0:T(8,128)(2,1)} %get-tuple-element.140, bf16[32,32,128]{2,1,0:T(8,128)(2,1)} %copy-done.5, bf16[32,1,256]{2,1,0:T(2,128)(2,1)S(1)} %collective-permute-done.7), kind=kLoop, calls=%fused_computation.262 | loop fusion | flops 2228224 | bytes 1114112 | tf_op jit(solution)/shard_map/concatenate | solution.py:18
  67.7 20.5 %collective-permute-done.9 = bf16[32,32,128]{2,1,0:T(8,128)(2,1)} collective-permute-done((bf16[32,32,128]{2,1,0:T(8,128)(2,1)}, bf16[32,32,128]{2,1,0:T(8,128)(2,1)}, u32[]{:S(2)}, u32[]{:S(2)}) %collective-permute-start.9) | collective-permute-done | bytes 262176 | tf_op jit(solution)/shard_map/ppermute | solution.py:10
  90.9 1.5 %collective-permute-start.11 = (bf16[32,1,256]{2,1,0:T(2,128)(2,1)S(1)}, bf16[32,1,256]{2,1,0:T(2,128)(2,1)S(1)}, u32[]{:S(2)}, u32[]{:S(2)}) collective-permute-start(bf16[32,1,256]{2,1,0:T(2,128)(2,1)S(1)} %get-tuple-element.209), channel_id=1, source_target_pairs={{1,0},{2,1},{3,2},{4,3},{5,4},{6,5},{7,6},{8,7},{9,8},{10,9},{11,1... | collective-permute-start | bytes 49160 | tf_op jit(solution)/shard_map/ppermute | solution.py:22
  93.7 5.8 %collective-permute-done.11 = bf16[32,1,256]{2,1,0:T(2,128)(2,1)S(1)} collective-permute-done((bf16[32,1,256]{2,1,0:T(2,128)(2,1)S(1)}, bf16[32,1,256]{2,1,0:T(2,128)(2,1)S(1)}, u32[]{:S(2)}, u32[]{:S(2)}) %collective-permute-start.11) | collective-permute-done | bytes 16416 | tf_op jit(solution)/shard_map/ppermute | solution.py:22
  99.5 1.4 %pad_maximum_fusion.3 = bf16[32,34,256]{2,1,0:T(8,128)(2,1)S(1)} fusion(bf16[32,1,256]{2,1,0:T(2,128)(2,1)S(1)} %collective-permute-done.11, bf16[32,32,128]{2,1,0:T(8,128)(2,1)} %get-tuple-element.143, bf16[32,32,128]{2,1,0:T(8,128)(2,1)} %copy-done.6, bf16[32,1,256]{2,1,0:T(2,128)(2,1)S(1)} %collective-permute-done.10), kind=kLoop, calls=%fused_computation.263 | loop fusion | flops 2228224 | bytes 1114112 | tf_op jit(solution)/shard_map/concatenate | solution.py:18
  100.9 8.1 %conditional.8 = ((bf16[32,32,128]{2,1,0:T(8,128)(2,1)}, f32[32,32,128]{2,1,0:T(8,128)S(1)}, bf16[2,32,32,128]{3,2,1,0:T(8,128)(2,1)})) conditional(s32[]{:T(128)} %convert_element_type.37, (bf16[32,32,128]{2,1,0:T(8,128)(2,1)}, f32[32,32,128]{2,1,0:T(8,128)S(1)}, bf16[2,32,32,128]{3,2,1,0:T(8,128)(2,1)}) %get-tuple-element.258, ...), branch_computations={%region_6.7_spmd, %region_7.8_spmd} | conditional | flops 2422472704 | bytes 54659140 | solution.py:66
  107.4 1.7 %constant_dynamic-update-slice_fusion.3 = bf16[2,32,32,128]{3,2,1,0:T(8,128)(2,1)} fusion(bf16[2,32,32,128]{3,2,1,0:T(8,128)(2,1)} %get-tuple-element.111, bf16[1,32,32,128]{3,2,1,0:T(8,128)(2,1)} %bitcast.91, s32[]{:T(128)S(6)} %select_n.38), kind=kLoop, calls=%fused_computation.207 | loop fusion | bytes 524292 | tf_op jit(solution)/shard_map/cond/branch_1_fun/jit(dynamic_update_index_in_dim)/dynamic_update_slice | solution.py:60
  110.3 7.9 %collective-permute-done.12 = bf16[32,32,128]{2,1,0:T(8,128)(2,1)} collective-permute-done((bf16[32,32,128]{2,1,0:T(8,128)(2,1)}, bf16[32,32,128]{2,1,0:T(8,128)(2,1)}, u32[]{:S(2)}, u32[]{:S(2)}) %collective-permute-start.12) | collective-permute-done | bytes 262176 | tf_op jit(solution)/shard_map/ppermute | solution.py:10
  120.9 1.5 %collective-permute-start.14 = (bf16[32,1,256]{2,1,0:T(2,128)(2,1)S(1)}, bf16[32,1,256]{2,1,0:T(2,128)(2,1)S(1)}, u32[]{:S(2)}, u32[]{:S(2)}) collective-permute-start(bf16[32,1,256]{2,1,0:T(2,128)(2,1)S(1)} %get-tuple-element.207), channel_id=1, source_target_pairs={{1,0},{2,1},{3,2},{4,3},{5,4},{6,5},{7,6},{8,7},{9,8},{10,9},{11,1... | collective-permute-start | bytes 49160 | tf_op jit(solution)/shard_map/ppermute | solution.py:22
  123.6 6.0 %collective-permute-done.14 = bf16[32,1,256]{2,1,0:T(2,128)(2,1)S(1)} collective-permute-done((bf16[32,1,256]{2,1,0:T(2,128)(2,1)S(1)}, bf16[32,1,256]{2,1,0:T(2,128)(2,1)S(1)}, u32[]{:S(2)}, u32[]{:S(2)}) %collective-permute-start.14) | collective-permute-done | bytes 16416 | tf_op jit(solution)/shard_map/ppermute | solution.py:22
  129.7 1.4 %pad_maximum_fusion.4 = bf16[32,34,256]{2,1,0:T(8,128)(2,1)S(1)} fusion(bf16[32,1,256]{2,1,0:T(2,128)(2,1)S(1)} %collective-permute-done.14, bf16[32,32,128]{2,1,0:T(8,128)(2,1)} %get-tuple-element.148, bf16[32,32,128]{2,1,0:T(8,128)(2,1)} %copy-done.3, bf16[32,1,256]{2,1,0:T(2,128)(2,1)S(1)} %collective-permute-done.13), kind=kLoop, calls=%fused_computation.264 | loop fusion | flops 2228224 | bytes 1114112 | tf_op jit(solution)/shard_map/concatenate | solution.py:18
  131.1 6.3 %conditional.9 = (f32[1,32,32,128]{3,2,1,0:T(8,128)S(1)}, bf16[1,2,32,32,128]{4,3,2,1,0:T(8,128)(2,1)}) conditional(s32[]{:T(128)} %convert_element_type.36, (f32[32,32,128]{2,1,0:T(8,128)S(1)}, bf16[2,32,32,128]{3,2,1,0:T(8,128)(2,1)}) %tuple.115, (bf16[32,34,256]{2,1,0:T(8,128)(2,1)S(1)}, bf16[9,256,512]{2,1,0:T(8,128)(2,1)S(1)}, ...), branch_computations={%region_8.9_spmd, %region_9.10_spmd} | conditional | flops 2422472704 | bytes 53610548 | solution.py:66
  (73 shorter events, 41.8 us)
Async XLA Ops:
  3.3 17.9 %copy-start = (bf16[1,9,256,512]{3,2,1,0:T(8,128)(2,1)S(1)}, bf16[1,9,256,512]{3,2,1,0:T(8,128)(2,1)}, u32[]{:S(2)}) copy-start(bf16[1,9,256,512]{3,2,1,0:T(8,128)(2,1)} %param.16) | copy-start | bytes 7077892
  3.3 17.9 %copy-start.8 = (f32[1,512]{1,0:T(1,128)S(1)}, f32[1,512]{1,0:T(1,128)}, u32[]{:S(2)}) copy-start(f32[1,512]{1,0:T(1,128)} %param.17) | copy-start | bytes 6148
  3.4 3.7 %collective-permute-start = (bf16[32,32,128]{2,1,0:T(8,128)(2,1)S(1)}, bf16[32,32,128]{2,1,0:T(8,128)(2,1)S(1)}, u32[]{:S(2)}, u32[]{:S(2)}) collective-permute-start(bf16[32,32,128]{2,1,0:T(8,128)(2,1)S(1)} %broadcast_in_dim.39), channel_id=1, source_target_pairs={{0,32},{32,64},{64,96},{1,33},{33,65},{65,97},{2,34},{34,66},{66,9... | collective-permute-start | bytes 786440 | tf_op jit(solution)/shard_map/ppermute | solution.py:10
  9.0 3.4 %collective-permute-start.1 = (bf16[32,1,256]{2,1,0:T(2,128)(2,1)S(1)}, bf16[32,1,256]{2,1,0:T(2,128)(2,1)S(1)}, u32[]{:S(2)}, u32[]{:S(2)}) collective-permute-start(bf16[32,1,256]{2,1,0:T(2,128)(2,1)S(1)} %get-tuple-element.214), channel_id=1, source_target_pairs={{0,1},{1,2},{2,3},{3,4},{4,5},{5,6},{6,7},{7,8},{8,9},{9,10},{10,1... | collective-permute-start | bytes 49160 | tf_op jit(solution)/shard_map/ppermute | solution.py:20
  11.4 8.5 %collective-permute-start.2 = (bf16[32,1,256]{2,1,0:T(2,128)(2,1)S(1)}, bf16[32,1,256]{2,1,0:T(2,128)(2,1)S(1)}, u32[]{:S(2)}, u32[]{:S(2)}) collective-permute-start(bf16[32,1,256]{2,1,0:T(2,128)(2,1)S(1)} %get-tuple-element.215), channel_id=1, source_target_pairs={{1,0},{2,1},{3,2},{4,3},{5,4},{6,5},{7,6},{8,7},{9,8},{10,9},{11,1... | collective-permute-start | bytes 49160 | tf_op jit(solution)/shard_map/ppermute | solution.py:22
  21.2 10.3 %copy-start.2 = (bf16[2,32,32,128]{3,2,1,0:T(8,128)(2,1)S(1)}, bf16[2,32,32,128]{3,2,1,0:T(8,128)(2,1)}, u32[]{:S(2)}) copy-start(bf16[2,32,32,128]{3,2,1,0:T(8,128)(2,1)} %param.15) | copy-start | bytes 1572868
  22.1 9.5 %collective-permute-start.3 = (bf16[32,32,128]{2,1,0:T(8,128)(2,1)}, bf16[32,32,128]{2,1,0:T(8,128)(2,1)}, u32[]{:S(2)}, u32[]{:S(2)}) collective-permute-start(bf16[32,32,128]{2,1,0:T(8,128)(2,1)} %get-tuple-element.137), channel_id=1, source_target_pairs={{0,32},{32,64},{64,96},{1,33},{33,65},{65,97},{2,34},{34,66},{66,9... | collective-permute-start | bytes 786440 | tf_op jit(solution)/shard_map/ppermute | solution.py:10
  32.6 0.7 copy-start.4
  34.2 2.8 %collective-permute-start.4 = (bf16[32,1,256]{2,1,0:T(2,128)(2,1)S(1)}, bf16[32,1,256]{2,1,0:T(2,128)(2,1)S(1)}, u32[]{:S(2)}, u32[]{:S(2)}) collective-permute-start(bf16[32,1,256]{2,1,0:T(2,128)(2,1)S(1)} %get-tuple-element.212), channel_id=1, source_target_pairs={{0,1},{1,2},{2,3},{3,4},{4,5},{5,6},{6,7},{7,8},{8,9},{9,10},{10,1... | collective-permute-start | bytes 49160 | tf_op jit(solution)/shard_map/ppermute | solution.py:20
  34.3 8.6 %collective-permute-start.5 = (bf16[32,1,256]{2,1,0:T(2,128)(2,1)S(1)}, bf16[32,1,256]{2,1,0:T(2,128)(2,1)S(1)}, u32[]{:S(2)}, u32[]{:S(2)}) collective-permute-start(bf16[32,1,256]{2,1,0:T(2,128)(2,1)S(1)} %get-tuple-element.213), channel_id=1, source_target_pairs={{1,0},{2,1},{3,2},{4,3},{5,4},{6,5},{7,6},{8,7},{9,8},{10,9},{11,1... | collective-permute-start | bytes 49160 | tf_op jit(solution)/shard_map/ppermute | solution.py:22
  44.3 9.2 %collective-permute-start.6 = (bf16[32,32,128]{2,1,0:T(8,128)(2,1)}, bf16[32,32,128]{2,1,0:T(8,128)(2,1)}, u32[]{:S(2)}, u32[]{:S(2)}) collective-permute-start(bf16[32,32,128]{2,1,0:T(8,128)(2,1)} %get-tuple-element.140), channel_id=1, source_target_pairs={{0,32},{32,64},{64,96},{1,33},{33,65},{65,97},{2,34},{34,66},{66,9... | collective-permute-start | bytes 786440 | tf_op jit(solution)/shard_map/ppermute | solution.py:10
  54.4 0.7 copy-start.5
  56.1 3.0 %collective-permute-start.7 = (bf16[32,1,256]{2,1,0:T(2,128)(2,1)S(1)}, bf16[32,1,256]{2,1,0:T(2,128)(2,1)S(1)}, u32[]{:S(2)}, u32[]{:S(2)}) collective-permute-start(bf16[32,1,256]{2,1,0:T(2,128)(2,1)S(1)} %get-tuple-element.210), channel_id=1, source_target_pairs={{0,1},{1,2},{2,3},{3,4},{4,5},{5,6},{6,7},{7,8},{8,9},{9,10},{10,1... | collective-permute-start | bytes 49160 | tf_op jit(solution)/shard_map/ppermute | solution.py:20
  56.3 8.6 %collective-permute-start.8 = (bf16[32,1,256]{2,1,0:T(2,128)(2,1)S(1)}, bf16[32,1,256]{2,1,0:T(2,128)(2,1)S(1)}, u32[]{:S(2)}, u32[]{:S(2)}) collective-permute-start(bf16[32,1,256]{2,1,0:T(2,128)(2,1)S(1)} %get-tuple-element.211), channel_id=1, source_target_pairs={{1,0},{2,1},{3,2},{4,3},{5,4},{6,5},{7,6},{8,7},{9,8},{10,9},{11,1... | collective-permute-start | bytes 49160 | tf_op jit(solution)/shard_map/ppermute | solution.py:22
  66.4 21.9 %collective-permute-start.9 = (bf16[32,32,128]{2,1,0:T(8,128)(2,1)}, bf16[32,32,128]{2,1,0:T(8,128)(2,1)}, u32[]{:S(2)}, u32[]{:S(2)}) collective-permute-start(bf16[32,32,128]{2,1,0:T(8,128)(2,1)} %get-tuple-element.143), channel_id=1, source_target_pairs={{0,32},{32,64},{64,96},{1,33},{33,65},{65,97},{2,34},{34,66},{66,9... | collective-permute-start | bytes 786440 | tf_op jit(solution)/shard_map/ppermute | solution.py:10
  89.2 0.7 copy-start.6
  90.8 2.8 %collective-permute-start.10 = (bf16[32,1,256]{2,1,0:T(2,128)(2,1)S(1)}, bf16[32,1,256]{2,1,0:T(2,128)(2,1)S(1)}, u32[]{:S(2)}, u32[]{:S(2)}) collective-permute-start(bf16[32,1,256]{2,1,0:T(2,128)(2,1)S(1)} %get-tuple-element.208), channel_id=1, source_target_pairs={{0,1},{1,2},{2,3},{3,4},{4,5},{5,6},{6,7},{7,8},{8,9},{9,10},{10,1... | collective-permute-start | bytes 49160 | tf_op jit(solution)/shard_map/ppermute | solution.py:20
  90.9 8.6 %collective-permute-start.11 = (bf16[32,1,256]{2,1,0:T(2,128)(2,1)S(1)}, bf16[32,1,256]{2,1,0:T(2,128)(2,1)S(1)}, u32[]{:S(2)}, u32[]{:S(2)}) collective-permute-start(bf16[32,1,256]{2,1,0:T(2,128)(2,1)S(1)} %get-tuple-element.209), channel_id=1, source_target_pairs={{1,0},{2,1},{3,2},{4,3},{5,4},{6,5},{7,6},{8,7},{9,8},{10,9},{11,1... | collective-permute-start | bytes 49160 | tf_op jit(solution)/shard_map/ppermute | solution.py:22
  109.0 9.1 %collective-permute-start.12 = (bf16[32,32,128]{2,1,0:T(8,128)(2,1)}, bf16[32,32,128]{2,1,0:T(8,128)(2,1)}, u32[]{:S(2)}, u32[]{:S(2)}) collective-permute-start(bf16[32,32,128]{2,1,0:T(8,128)(2,1)} %get-tuple-element.148), channel_id=1, source_target_pairs={{0,32},{32,64},{64,96},{1,33},{33,65},{65,97},{2,34},{34,66},{66,9... | collective-permute-start | bytes 786440 | tf_op jit(solution)/shard_map/ppermute | solution.py:10
  119.2 0.7 copy-start.3
  120.8 2.8 %collective-permute-start.13 = (bf16[32,1,256]{2,1,0:T(2,128)(2,1)S(1)}, bf16[32,1,256]{2,1,0:T(2,128)(2,1)S(1)}, u32[]{:S(2)}, u32[]{:S(2)}) collective-permute-start(bf16[32,1,256]{2,1,0:T(2,128)(2,1)S(1)} %get-tuple-element.206), channel_id=1, source_target_pairs={{0,1},{1,2},{2,3},{3,4},{4,5},{5,6},{6,7},{7,8},{8,9},{9,10},{10,1... | collective-permute-start | bytes 49160 | tf_op jit(solution)/shard_map/ppermute | solution.py:20
  120.9 8.8 %collective-permute-start.14 = (bf16[32,1,256]{2,1,0:T(2,128)(2,1)S(1)}, bf16[32,1,256]{2,1,0:T(2,128)(2,1)S(1)}, u32[]{:S(2)}, u32[]{:S(2)}) collective-permute-start(bf16[32,1,256]{2,1,0:T(2,128)(2,1)S(1)} %get-tuple-element.207), channel_id=1, source_target_pairs={{1,0},{2,1},{3,2},{4,3},{5,4},{6,5},{7,6},{8,7},{9,8},{10,9},{11,1... | collective-permute-start | bytes 49160 | tf_op jit(solution)/shard_map/ppermute | solution.py:22
  137.4 0.8 copy-start.1
where the time goes:
time: 139 us; the launch traced here: 138 us
  waiting for transfers between devices  83 us (60%)
  other arithmetic  18.5 us (13%)
  starting transfers between devices  15.2 us (11%)
  local copies, waits for them, and re-layouts  11.7 us (8%)
  matrix products  8.81 us (6%)
    ppermute x5, waiting for transfers between devices, passed_along(): return lax.ppermute(value, axis, pairs)  46.7 us
    ppermute x5, waiting for transfers between devices, extended(): lax.ppermute(head, axis, [((i + 1) % count, i) for i in range(count)])  30.9 us
    dot_general x18, matrix products, convolve(): jnp.dot(window_block, weight[offset], preferred_element_type=jnp.float32)  8.81 us
    unnamed x20, local copies, waits for them, and re-layouts  7.13 us
    concatenate x5, other arithmetic, extended(): jnp.concatenate([lax.ppermute(tail, axis, [(i, (i + 1) % count) for i in...  7.11 us
    ppermute x5, starting transfers between devices, passed_along(): return lax.ppermute(value, axis, pairs)  6.57 us
    ppermute x5, starting transfers between devices, extended(): lax.ppermute(head, axis, [((i + 1) % count, i) for i in range(count)])  5.81 us
    ppermute x5, waiting for transfers between devices, extended(): lax.ppermute(tail, axis, [(i, (i + 1) % count) for i in range(count)])  5.38 us
  transfers between devices with their start and end apart: 15, of which 15 were waited for; matrix products, arithmetic and copies ran while one was open for 1% of the time, Pallas kernels for 0%

commit v1 on v0

v1 whole, which is shorter than its diff:
```python
import jax
import jax.numpy as jnp
from jax import lax
from jax.experimental import pallas as pl
from jax.experimental.pallas import tpu as pltpu
from jax.sharding import PartitionSpec as P

MESH = pl.DeviceIdType.MESH
PAD = 8
WIDTH = 48
EDGE = 5
CELL_EDGE = 4
ORDER = ((0, 0), (0, 1), (1, 0), (0, 2), (0, 3), (1, 1), (1, 2), (1, 3))


def row_shifts(columns):
    blank = jnp.zeros((columns.shape[0], 1, columns.shape[2]), columns.dtype)
    above = jnp.concatenate([blank, columns[:, :-1]], axis=1)
    below = jnp.concatenate([columns[:, 1:], blank], axis=1)
    return above, below


def gate_update(gate_sums, memory):
    chans = memory.shape[-1]
    ingate = 0.5 * jnp.tanh(0.5 * gate_sums[:, :chans]) + 0.5
    forget = 0.5 * jnp.tanh(0.5 * gate_sums[:, chans : 2 * chans]) + 0.5
    candidate = jnp.tanh(gate_sums[:, 2 * chans : 3 * chans])
    outgate = 0.5 * jnp.tanh(0.5 * gate_sums[:, 3 * chans :]) + 0.5
    new_memory = forget * memory + ingate * candidate
    return outgate * jnp.tanh(new_memory), new_memory


def kernel(
    layers, sectors,
    frames, weights, biases, hidden_init, cell_init, hidden_out, cell_out,
    w, bias, stage_h, stage_c, stage_u, hc, hs, uc, us, cells, out_h, out_c,
    load_sem, w_sem, edge_send, edge_recv, next_send, next_recv, out_sem,
):
    layer, sector = lax.axis_index("layer"), lax.axis_index("lon")
    right, left = lax.rem(sector + 1, sectors), lax.rem(sector + sectors - 1, sectors)
    steps, rows, cols, chans = stage_u.shape

    load_h = pltpu.make_async_copy(hidden_init.at[0], stage_h, load_sem.at[0])
    load_c = pltpu.make_async_copy(cell_init.at[0], stage_c, load_sem.at[1])
    load_u = [pltpu.make_async_copy(frames.at[t], stage_u.at[t], load_sem.at[2 + t]) for t in range(steps)]
    load_b = pltpu.make_async_copy(biases, bias, load_sem.at[4])
    load_w = [pltpu.make_async_copy(weights.at[0, i], w.at[i], w_sem.at[i]) for i in range(9)]
    load_h.start()

    @pl.when(layer == 0)
    def _():
        load_u[0].start()

    load_c.start()
    for copy in load_w:
        copy.start()
    load_b.start()

    @pl.when(layer == 0)
    def _():
        load_u[1].start()

    barrier = pltpu.get_barrier_semaphore()
    for side in (left, right):
        pl.semaphore_signal(barrier, inc=1, device_id=(layer, side), device_id_type=MESH)

    @pl.when(layer > 0)
    def _():
        pl.semaphore_signal(barrier, inc=1, device_id=(layer - 1, sector), device_id_type=MESH)

    def edge_copies(index, buffer, width):
        out = []
        for side, source, target, which in (
            (right, PAD + cols - width, PAD - width, 0),
            (left, PAD, PAD + cols, 1),
        ):
            out.append(
                pltpu.make_async_remote_copy(
                    src_ref=buffer.at[pl.ds(source, width)],
                    dst_ref=buffer.at[pl.ds(target, width)],
                    send_sem=edge_send.at[2 * index + which],
                    recv_sem=edge_recv.at[2 * index + which],
                    device_id=(layer, side),
                    device_id_type=MESH,
                )
            )
        return out

    edges_h = edge_copies(0, hc.at[0], EDGE)
    edges_c = edge_copies(1, cells.at[0], CELL_EDGE)
    edges_u = [edge_copies(2 + t, uc.at[t], EDGE) for t in range(steps)]

    def shift_into(center, shifted, start, count):
        above, below = row_shifts(center[pl.ds(start, count)])
        shifted[0, pl.ds(start, count)] = above
        shifted[1, pl.ds(start, count)] = below

    load_h.wait()
    hc[0, pl.ds(PAD, cols)] = jnp.swapaxes(stage_h[...], 0, 1)

    @pl.when(layer < layers - 1)
    def _():
        pl.semaphore_wait(barrier, 3)

    @pl.when(layer == layers - 1)
    def _():
        pl.semaphore_wait(barrier, 2)

    for copy in edges_h:
        copy.start()

    @pl.when(layer == 0)
    def _():
        load_u[0].wait()
        uc[0, pl.ds(PAD, cols)] = jnp.swapaxes(stage_u[0], 0, 1)
        for copy in edges_u[0]:
            copy.start()

    load_c.wait()
    cells[0, pl.ds(PAD, cols)] = jnp.swapaxes(stage_c[...], 0, 1)
    for copy in edges_c:
        copy.start()

    shift_into(hc.at[0], hs.at[0], PAD, cols)

    @pl.when(layer == 0)
    def _():
        shift_into(uc.at[0], us.at[0], PAD, cols)
        load_u[1].wait()
        uc[1, pl.ds(PAD, cols)] = jnp.swapaxes(stage_u[1], 0, 1)
        for copy in edges_u[1]:
            copy.start()
        shift_into(uc.at[1], us.at[1], PAD, cols)

    def finish_edges():
        for copy in edges_h + edges_c:
            copy.wait_recv()
        shift_into(hc.at[0], hs.at[0], PAD - EDGE, EDGE)
        shift_into(hc.at[0], hs.at[0], PAD + cols, EDGE)

        @pl.when(layer == 0)
        def _():
            for t in range(steps):
                for copy in edges_u[t]:
                    copy.wait_recv()
                shift_into(uc.at[t], us.at[t], PAD - EDGE, EDGE)
                shift_into(uc.at[t], us.at[t], PAD + cols, EDGE)

    def spans(depth, k):
        if k == 0:
            return (PAD + 8 + depth, PAD + 16 - depth), 8
        return (PAD + 8 + depth - 4 * k, PAD + 20 - depth + 4 * k), 4

    def sends(t, k, depth):
        if k == 0:
            pieces = ((PAD + 8 + depth, 16 - 2 * depth),)
        else:
            starts, count = spans(depth, k)
            pieces = tuple((start, count) for start in starts)
        return [
            pltpu.make_async_remote_copy(
                src_ref=hc.at[t + 1, pl.ds(start, count)],
                dst_ref=uc.at[t, pl.ds(start, count)],
                send_sem=next_send.at[t, k, i],
                recv_sem=next_recv.at[t, k, i],
                device_id=(layer + 1, sector),
                device_id_type=MESH,
            )
            for i, (start, count) in enumerate(pieces)
        ], pieces

    def receive(t, k):
        if k == 0:
            for source in range(layers - 1):

                @pl.when(layer == source + 1)
                def _():
                    copies, pieces = sends(t, 0, source + t)
                    copies[0].wait_recv()
                    shift_into(uc.at[t], us.at[t], *pieces[0])
        else:

            @pl.when(layer > 0)
            def _():
                copies, pieces = sends(t, k, layer - 1 + t)
                for copy, piece in zip(copies, pieces):
                    copy.wait_recv()
                    shift_into(uc.at[t], us.at[t], *piece)

    def forward(t, k, act):
        if k == 0:
            for source in range(layers - 1):

                @pl.when(layer == source)
                def _():
                    for copy in sends(t, 0, source + t)[0]:
                        act(copy)
        else:

            @pl.when(layer < layers - 1)
            def _():
                for copy in sends(t, k, layer + t)[0]:
                    act(copy)

    def compute(t, k):
        depth = layer + t
        starts, count = spans(depth, k)
        flat = count * rows

        def window(center, shifted, a, b):
            pick = {0: lambda s: shifted[0, s], 1: lambda s: center[s], 2: lambda s: shifted[1, s]}[a]
            return jnp.concatenate(
                [pick(pl.ds(start + b - 1, count)).reshape(flat, chans) for start in starts], axis=0
            )

        patches = jnp.concatenate(
            [
                part
                for a in range(3)
                for b in range(3)
                for part in (
                    window(uc.at[t], us.at[t], a, b),
                    window(hc.at[t], hs.at[t], a, b),
                )
            ],
            axis=1,
        )
        sums = jnp.dot(patches, w[...].reshape(18 * chans, 4 * chans), preferred_element_type=jnp.float32)
        sums = sums + bias[...]
        memory = jnp.concatenate([cells[t, pl.ds(start, count)].reshape(flat, chans) for start in starts], axis=0)
        hidden, memory = gate_update(sums, memory)
        hidden = hidden.astype(jnp.bfloat16).reshape(2, count, rows, chans)
        memory = memory.reshape(2, count, rows, chans)
        for i, start in enumerate(starts):
            cells[t + 1, pl.ds(start, count)] = memory[i]
            hc[t + 1, pl.ds(start, count)] = hidden[i]
        forward(t, k, lambda copy: copy.start())
        if t + 1 < steps:
            for i, start in enumerate(starts):
                above, below = row_shifts(hidden[i])
                hs[t + 1, 0, pl.ds(start, count)] = above
                hs[t + 1, 1, pl.ds(start, count)] = below

    store_h = [pltpu.make_async_copy(out_h.at[t], hidden_out.at[0, t], out_sem.at[t]) for t in range(steps)]
    store_c = pltpu.make_async_copy(out_c, cell_out.at[0], out_sem.at[steps])

    for copy in load_w:
        copy.wait()
    load_b.wait()
    for t, k in ORDER:
        if (t, k) == (0, 2):
            finish_edges()
        receive(t, k)
        compute(t, k)
        if k == 3:
            out_h[t] = jnp.swapaxes(hc[t + 1, pl.ds(PAD, cols)], 0, 1)
            store_h[t].start()
    out_c[...] = jnp.swapaxes(cells[steps, pl.ds(PAD, cols)], 0, 1)
    store_c.start()

    for copy in edges_h + edges_c:
        copy.wait_send()

    @pl.when(layer == 0)
    def _():
        for copies in edges_u:
            for copy in copies:
                copy.wait_send()

    for t, k in ORDER:
        forward(t, k, lambda copy: copy.wait_send())
    for copy in store_h + [store_c]:
        copy.wait()


def solution(mesh):
    layers, sectors = mesh.shape["layer"], mesh.shape["lon"]

    def local(frames, weights, biases, hidden_init, cell_init):
        steps, rows, cols, chans = frames.shape
        bf16, f32 = jnp.bfloat16, jnp.float32
        any_space = pl.BlockSpec(memory_space=pl.ANY)
        return pl.pallas_call(
            lambda *refs: kernel(layers, sectors, *refs),
            out_shape=[
                jax.ShapeDtypeStruct((1, steps, rows, cols, chans), bf16),
                jax.ShapeDtypeStruct((1, rows, cols, chans), f32),
            ],
            in_specs=[any_space] * 5,
            out_specs=[any_space] * 2,
            scratch_shapes=[
                pltpu.VMEM((9, 2 * chans, 4 * chans), bf16),
                pltpu.VMEM((1, 4 * chans), f32),
                pltpu.VMEM((rows, cols, chans), bf16),
                pltpu.VMEM((rows, cols, chans), f32),
                pltpu.VMEM((steps, rows, cols, chans), bf16),
                pltpu.VMEM((steps + 1, WIDTH, rows, chans), bf16),
                pltpu.VMEM((steps, 2, WIDTH, rows, chans), bf16),
                pltpu.VMEM((steps, WIDTH, rows, chans), bf16),
                pltpu.VMEM((steps, 2, WIDTH, rows, chans), bf16),
                pltpu.VMEM((steps + 1, WIDTH, rows, chans), f32),
                pltpu.VMEM((steps, rows, cols, chans), bf16),
                pltpu.VMEM((rows, cols, chans), f32),
                pltpu.SemaphoreType.DMA((5,)),
                pltpu.SemaphoreType.DMA((9,)),
                pltpu.SemaphoreType.DMA((8,)),
                pltpu.SemaphoreType.DMA((8,)),
                pltpu.SemaphoreType.DMA((steps, 4, 2)),
                pltpu.SemaphoreType.DMA((steps, 4, 2)),
                pltpu.SemaphoreType.DMA((steps + 1,)),
            ],
            compiler_params=pltpu.CompilerParams(
                collective_id=0, has_side_effects=True, vmem_limit_bytes=48 * 1024 * 1024
            ),
            name="conv_lstm",
        )(frames, weights, biases, hidden_init, cell_init)

    in_specs = (
        P(None, None, "lon", None),
        P("layer", None, None, None),
        P("layer", None),
        P("layer", None, "lon", None),
        P("layer", None, "lon", None),
    )
    out_specs = (P("layer", None, None, "lon", None), P("layer", None, "lon", None))
    return jax.shard_map(local, mesh=mesh, in_specs=in_specs, out_specs=out_specs, check_vma=False)
```

time: 139 us -> 36.4 us (0.26)
  the two profiles are of different devices: /device:TPU:63 before, /device:TPU:33 now
where the time goes in v1:
time: 36.4 us; the launch traced here: 36.1 us
  Pallas kernels  28.5 us (78%)
  local copies, waits for them, and re-layouts  6.96 us (19%)
  between operations  0.65 us (2%)
    pallas_call x1, Pallas kernels, local(): pl.pallas_call(lambda *refs: kernel(layers, sectors, *refs), out_shape=[j...  28.5 us
    unnamed x12, local copies, waits for them, and re-layouts  6.96 us

profile of v1, /device:TPU:33, one launch (start us, length us, event | category | flops | bytes accessed | tf_op | source)
XLA Modules:
  0.0 36.1 jit_solution(4841457134643404964)
XLA Ops:
  0.6 0.0 copy-start
  0.6 1.7 %copy-done = bf16[1,9,256,512]{3,2,1,0:T(8,128)(2,1)S(1)} copy-done((bf16[1,9,256,512]{3,2,1,0:T(8,128)(2,1)S(1)}, bf16[1,9,256,512]{3,2,1,0:T(8,128)(2,1)}, u32[]{:S(2)}) %copy-start) | copy-done | bytes 2359320
  2.3 0.0 copy-start.1
  2.3 1.0 %copy-done.1 = bf16[2,32,32,128]{3,2,1,0:T(8,128)(2,1)S(1)} copy-done((bf16[2,32,32,128]{3,2,1,0:T(8,128)(2,1)S(1)}, bf16[2,32,32,128]{3,2,1,0:T(8,128)(2,1)}, u32[]{:S(2)}) %copy-start.1) | copy-done | bytes 524312
  3.3 0.0 copy-start.2
  3.3 1.0 %copy-done.2 = f32[1,32,32,128]{3,2,1,0:T(8,128)S(1)} copy-done((f32[1,32,32,128]{3,2,1,0:T(8,128)S(1)}, f32[1,32,32,128]{3,2,1,0:T(8,128)}, u32[]{:S(2)}) %copy-start.2) | copy-done | bytes 524312
  4.4 0.0 copy-start.3
  4.4 0.9 %copy-done.3 = bf16[1,32,32,128]{3,2,1,0:T(8,128)(2,1)S(1)} copy-done((bf16[1,32,32,128]{3,2,1,0:T(8,128)(2,1)S(1)}, bf16[1,32,32,128]{3,2,1,0:T(8,128)(2,1)}, u32[]{:S(2)}) %copy-start.3) | copy-done | bytes 262168
  5.3 0.0 copy-start.4
  5.3 0.7 %copy-done.4 = f32[1,512]{1,0:T(1,128)S(1)} copy-done((f32[1,512]{1,0:T(1,128)S(1)}, f32[1,512]{1,0:T(1,128)}, u32[]{:S(2)}) %copy-start.4) | copy-done | bytes 2072
  6.0 28.5 %conv_lstm.1 = (bf16[1,2,32,32,128]{4,3,2,1,0:T(8,128)(2,1)S(1)}, f32[1,32,32,128]{3,2,1,0:T(8,128)S(1)}) custom-call(bf16[2,32,32,128]{3,2,1,0:T(8,128)(2,1)S(1)} %copy-done.1, bf16[1,9,256,512]{3,2,1,0:T(8,128)(2,1)S(1)} %copy-done, f32[1,512]{1,0:T(1,128)S(1)} %copy-done.4, bf16[1,32,32,128]{3,2,1,0:T(8,128)(2,1)S(1)} %copy-done.3, ...), custom_call_target="tpu_custom_call" | custom-call | tf_op jit(solution)/shard_map/conv_lstm/pallas_call | solution.py:283
  34.6 0.8 %copy.9 = bf16[1,2,32,32,128]{4,3,2,1,0:T(8,128)(2,1)} copy(bf16[1,2,32,32,128]{4,3,2,1,0:T(8,128)(2,1)S(1)} %get-tuple-element.4) | data formatting | bytes 1048576
  35.4 0.8 %copy.10 = f32[1,32,32,128]{3,2,1,0:T(8,128)} copy(f32[1,32,32,128]{3,2,1,0:T(8,128)S(1)} %get-tuple-element.5) | data formatting | bytes 1048576
Async XLA Ops:
  0.6 1.7 %copy-start = (bf16[1,9,256,512]{3,2,1,0:T(8,128)(2,1)S(1)}, bf16[1,9,256,512]{3,2,1,0:T(8,128)(2,1)}, u32[]{:S(2)}) copy-start(bf16[1,9,256,512]{3,2,1,0:T(8,128)(2,1)} %refs_1_.1) | copy-start | bytes 7077892
  2.3 1.0 %copy-start.1 = (bf16[2,32,32,128]{3,2,1,0:T(8,128)(2,1)S(1)}, bf16[2,32,32,128]{3,2,1,0:T(8,128)(2,1)}, u32[]{:S(2)}) copy-start(bf16[2,32,32,128]{3,2,1,0:T(8,128)(2,1)} %refs_0_.1) | copy-start | bytes 1572868
  3.3 1.0 %copy-start.2 = (f32[1,32,32,128]{3,2,1,0:T(8,128)S(1)}, f32[1,32,32,128]{3,2,1,0:T(8,128)}, u32[]{:S(2)}) copy-start(f32[1,32,32,128]{3,2,1,0:T(8,128)} %refs_4_.1) | copy-start | bytes 1572868
  4.4 0.9 %copy-start.3 = (bf16[1,32,32,128]{3,2,1,0:T(8,128)(2,1)S(1)}, bf16[1,32,32,128]{3,2,1,0:T(8,128)(2,1)}, u32[]{:S(2)}) copy-start(bf16[1,32,32,128]{3,2,1,0:T(8,128)(2,1)} %refs_3_.1) | copy-start | bytes 786436
  5.3 0.7 %copy-start.4 = (f32[1,512]{1,0:T(1,128)S(1)}, f32[1,512]{1,0:T(1,128)}, u32[]{:S(2)}) copy-start(f32[1,512]{1,0:T(1,128)} %refs_2_.1) | copy-start | bytes 6148

commit v2 on v1

v2 whole, which is shorter than its diff:
```python
import jax
import jax.numpy as jnp
from jax import lax
from jax.experimental import pallas as pl
from jax.experimental.pallas import tpu as pltpu
from jax.sharding import PartitionSpec as P

MESH = pl.DeviceIdType.MESH
PAD = 8
WIDTH = 48
EDGE = 5
CELL_EDGE = 4
ORDER = ((0, "mid"), (0, "near"), (1, "mid"), (1, "near"), (0, "east"), (1, "east"), (0, "west"), (1, "west"))
CHUNKS = ("mid", "near", "east", "west")


def spans(depth, chunk):
    if chunk == "mid":
        return (PAD + 8 + depth, PAD + 16 - depth), 8
    if chunk == "near":
        return (PAD + 1 + depth, PAD + 24 - depth), 7
    if chunk == "east":
        return (PAD + 31 - depth,), 5
    return (PAD - 4 + depth,), 5


def row_shifts(columns):
    blank = jnp.zeros((columns.shape[0], 1, columns.shape[2]), columns.dtype)
    above = jnp.concatenate([blank, columns[:, :-1]], axis=1)
    below = jnp.concatenate([columns[:, 1:], blank], axis=1)
    return above, below


def gate_update(gate_sums, memory):
    chans = memory.shape[-1]
    ingate = 0.5 * jnp.tanh(0.5 * gate_sums[:, :chans]) + 0.5
    forget = 0.5 * jnp.tanh(0.5 * gate_sums[:, chans : 2 * chans]) + 0.5
    candidate = jnp.tanh(gate_sums[:, 2 * chans : 3 * chans])
    outgate = 0.5 * jnp.tanh(0.5 * gate_sums[:, 3 * chans :]) + 0.5
    new_memory = forget * memory + ingate * candidate
    return outgate * jnp.tanh(new_memory), new_memory


def kernel(
    layers, sectors,
    frames, weights, biases, hidden_init, cell_init, h_new, cell_new,
    w, bias, stage_h, stage_c, stage_u, h_old, hs, uc, us, cell_old, cell_mid,
    load_sem, w_sem, edge_send, edge_recv, next_send, next_recv, late_sem,
):
    layer, sector = lax.axis_index("layer"), lax.axis_index("lon")
    right, left = lax.rem(sector + 1, sectors), lax.rem(sector + sectors - 1, sectors)
    steps, rows, cols, chans = stage_u.shape
    first, last = sector == 0, sector == sectors - 1
    h_at = [h_old] + [h_new.at[t] for t in range(steps)]
    cell_at = [cell_old, cell_mid, cell_new]

    load_h = pltpu.make_async_copy(hidden_init.at[0], stage_h, load_sem.at[0])
    load_c = pltpu.make_async_copy(cell_init.at[0], stage_c, load_sem.at[1])
    load_u = [pltpu.make_async_copy(frames.at[t], stage_u.at[t], load_sem.at[2 + t]) for t in range(steps)]
    load_b = pltpu.make_async_copy(biases, bias, load_sem.at[4])
    load_w = [pltpu.make_async_copy(weights.at[0, i], w.at[i], w_sem.at[i]) for i in range(9)]

    barrier = pltpu.get_barrier_semaphore()
    load_h.start()

    @pl.when(layer == 0)
    def _():
        load_u[0].start()

    pl.semaphore_signal(barrier, inc=1, device_id=(layer, left), device_id_type=MESH)

    @pl.when(jnp.logical_not(last))
    def _():
        pl.semaphore_signal(barrier, inc=1, device_id=(layer, right), device_id_type=MESH)

    @pl.when(layer > 0)
    def _():
        pl.semaphore_signal(barrier, inc=1, device_id=(layer - 1, sector), device_id_type=MESH)

    load_c.start()

    @pl.when(layer == 0)
    def _():
        load_u[1].start()

    load_b.start()
    for copy in load_w:
        copy.start()

    def edge_copies(index, buffer, width):
        return [
            pltpu.make_async_remote_copy(
                src_ref=buffer.at[pl.ds(source, width)],
                dst_ref=buffer.at[pl.ds(target, width)],
                send_sem=edge_send.at[2 * index + which],
                recv_sem=edge_recv.at[2 * index + which],
                device_id=(layer, side),
                device_id_type=MESH,
            )
            for side, source, target, which in (
                (right, PAD + cols - width, PAD - width, 0),
                (left, PAD, PAD + cols, 1),
            )
        ]

    edges_h = edge_copies(0, h_old, EDGE)
    edges_c = edge_copies(1, cell_old, CELL_EDGE)
    edges_u = [edge_copies(2 + t, uc.at[t], EDGE) for t in range(steps)]

    def send_edges(edges):
        edges[0].start()

        @pl.when(jnp.logical_not(first))
        def _():
            edges[1].start()

    def place(target, staged, start, stop):
        target[pl.ds(PAD + start, stop - start)] = jnp.swapaxes(staged[:, start:stop], 0, 1)

    def place_ends(target, staged):
        place(target, staged, 0, 8)
        place(target, staged, cols - 8, cols)

    def shift_into(center, shifted, start, count):
        above, below = row_shifts(center[pl.ds(start, count)])
        shifted[0, pl.ds(start, count)] = above
        shifted[1, pl.ds(start, count)] = below

    load_h.wait()
    place_ends(h_old, stage_h)
    awaited = 3 - (layer == layers - 1).astype(jnp.int32) - first.astype(jnp.int32)
    pl.semaphore_wait(barrier, awaited)

    @pl.when(last)
    def _():
        pl.semaphore_signal(late_sem, inc=1, device_id=(layer, right), device_id_type=MESH)

    send_edges(edges_h)

    @pl.when(layer == 0)
    def _():
        load_u[0].wait()
        place_ends(uc.at[0], stage_u.at[0])
        send_edges(edges_u[0])

    load_c.wait()
    place_ends(cell_old, stage_c)
    send_edges(edges_c)

    @pl.when(layer == 0)
    def _():
        load_u[1].wait()
        place_ends(uc.at[1], stage_u.at[1])
        send_edges(edges_u[1])

    place(h_old, stage_h, 8, cols - 8)
    place(cell_old, stage_c, 8, cols - 8)
    shift_into(h_old, hs.at[0], PAD, cols)

    @pl.when(layer == 0)
    def _():
        for t in range(steps):
            place(uc.at[t], stage_u.at[t], 8, cols - 8)
            shift_into(uc.at[t], us.at[t], PAD, cols)

    def finish_edges(which):
        start = (PAD - EDGE, PAD + cols)[which]
        edges_h[which].wait_recv()
        edges_c[which].wait_recv()
        shift_into(h_old, hs.at[0], start, EDGE)

        @pl.when(layer == 0)
        def _():
            for t in range(steps):
                edges_u[t][which].wait_recv()
                shift_into(uc.at[t], us.at[t], start, EDGE)

    def to_next(t, chunk, pieces):
        return [
            pltpu.make_async_remote_copy(
                src_ref=h_new.at[t, pl.ds(start, count)],
                dst_ref=uc.at[t, pl.ds(start, count)],
                send_sem=next_send.at[t, CHUNKS.index(chunk), i],
                recv_sem=next_recv.at[t, CHUNKS.index(chunk), i],
                device_id=(layer + 1, sector),
                device_id_type=MESH,
            )
            for i, (start, count) in enumerate(pieces)
        ]

    def each_piece(t, chunk, source, act):
        if chunk == "mid":
            for known in range(layers - 1):

                @pl.when(source == known)
                def _():
                    pieces = ((PAD + 8 + known + t, 16 - 2 * (known + t)),)
                    for copy, piece in zip(to_next(t, chunk, pieces), pieces):
                        act(copy, piece)
        else:

            @pl.when(jnp.logical_and(source >= 0, source < layers - 1))
            def _():
                starts, count = spans(source + t, chunk)
                pieces = tuple((start, count) for start in starts)
                for copy, piece in zip(to_next(t, chunk, pieces), pieces):
                    act(copy, piece)

    def receive(t, chunk):
        def act(copy, piece):
            copy.wait_recv()
            shift_into(uc.at[t], us.at[t], *piece)

        each_piece(t, chunk, layer - 1, act)

    def compute(t, chunk):
        starts, count = spans(layer + t, chunk)
        flat = count * rows

        def window(center, shifted, a, b):
            pick = (lambda s: shifted[0, s], lambda s: center[s], lambda s: shifted[1, s])[a]
            return jnp.concatenate(
                [pick(pl.ds(start + b - 1, count)).reshape(flat, chans) for start in starts], axis=0
            )

        patches = jnp.concatenate(
            [
                part
                for a in range(3)
                for b in range(3)
                for part in (
                    window(uc.at[t], us.at[t], a, b),
                    window(h_at[t], hs.at[t], a, b),
                )
            ],
            axis=1,
        )
        sums = jnp.dot(patches, w[...].reshape(18 * chans, 4 * chans), preferred_element_type=jnp.float32)
        sums = sums + bias[...]
        memory = jnp.concatenate([cell_at[t][pl.ds(start, count)].reshape(flat, chans) for start in starts], axis=0)
        hidden, memory = gate_update(sums, memory)
        hidden = hidden.astype(jnp.bfloat16).reshape(len(starts), count, rows, chans)
        memory = memory.reshape(len(starts), count, rows, chans)
        for i, start in enumerate(starts):
            h_new[t, pl.ds(start, count)] = hidden[i]
            cell_at[t + 1][pl.ds(start, count)] = memory[i]
        each_piece(t, chunk, layer, lambda copy, piece: copy.start())
        if t + 1 < steps:
            for i, start in enumerate(starts):
                above, below = row_shifts(hidden[i])
                hs[t + 1, 0, pl.ds(start, count)] = above
                hs[t + 1, 1, pl.ds(start, count)] = below

    for copy in load_w:
        copy.wait()
    load_b.wait()
    for t, chunk in ORDER:
        if (t, chunk) == (0, "east"):

            @pl.when(first)
            def _():
                pl.semaphore_wait(late_sem, 1)
                for edges in (edges_h, edges_c):
                    edges[1].start()

                @pl.when(layer == 0)
                def _():
                    for edges in edges_u:
                        edges[1].start()

            finish_edges(1)
        if (t, chunk) == (0, "west"):
            finish_edges(0)
        receive(t, chunk)
        compute(t, chunk)

    for copy in edges_h + edges_c:
        copy.wait_send()

    @pl.when(layer == 0)
    def _():
        for edges in edges_u:
            for copy in edges:
                copy.wait_send()

    for t, chunk in ORDER:
        each_piece(t, chunk, layer, lambda copy, piece: copy.wait_send())


def finish(h_ref, cell_ref, hidden_out, cell_out, out_h, out_c, sems):
    steps, rows, cols, chans = out_h.shape
    copies = []
    for t in range(steps):
        out_h[t] = jnp.swapaxes(h_ref[t, pl.ds(PAD, cols)], 0, 1)
        copies.append(pltpu.make_async_copy(out_h.at[t], hidden_out.at[0, t], sems.at[t]))
        copies[-1].start()
    out_c[...] = jnp.swapaxes(cell_ref[pl.ds(PAD, cols)], 0, 1)
    copies.append(pltpu.make_async_copy(out_c, cell_out.at[0], sems.at[steps]))
    copies[-1].start()
    for copy in copies:
        copy.wait()


def solution(mesh):
    layers, sectors = mesh.shape["layer"], mesh.shape["lon"]

    def local(frames, weights, biases, hidden_init, cell_init):
        steps, rows, cols, chans = frames.shape
        bf16, f32 = jnp.bfloat16, jnp.float32
        in_hbm = pl.BlockSpec(memory_space=pltpu.HBM)
        in_vmem = pl.BlockSpec(memory_space=pltpu.VMEM)
        operands = [
            pltpu.with_memory_space_constraint(x, pltpu.HBM)
            for x in (frames, weights, biases, hidden_init, cell_init)
        ]
        hidden, memory = pl.pallas_call(
            lambda *refs: kernel(layers, sectors, *refs),
            out_shape=[
                pltpu.VMEM((steps, WIDTH, rows, chans), bf16),
                pltpu.VMEM((WIDTH, rows, chans), f32),
            ],
            in_specs=[in_hbm] * 5,
            out_specs=[in_vmem] * 2,
            scratch_shapes=[
                pltpu.VMEM((9, 2 * chans, 4 * chans), bf16),
                pltpu.VMEM((1, 4 * chans), f32),
                pltpu.VMEM((rows, cols, chans), bf16),
                pltpu.VMEM((rows, cols, chans), f32),
                pltpu.VMEM((steps, rows, cols, chans), bf16),
                pltpu.VMEM((WIDTH, rows, chans), bf16),
                pltpu.VMEM((steps, 2, WIDTH, rows, chans), bf16),
                pltpu.VMEM((steps, WIDTH, rows, chans), bf16),
                pltpu.VMEM((steps, 2, WIDTH, rows, chans), bf16),
                pltpu.VMEM((WIDTH, rows, chans), f32),
                pltpu.VMEM((WIDTH, rows, chans), f32),
                pltpu.SemaphoreType.DMA((5,)),
                pltpu.SemaphoreType.DMA((9,)),
                pltpu.SemaphoreType.DMA((8,)),
                pltpu.SemaphoreType.DMA((8,)),
                pltpu.SemaphoreType.DMA((steps, 4, 2)),
                pltpu.SemaphoreType.DMA((steps, 4, 2)),
                pltpu.SemaphoreType.REGULAR,
            ],
            compiler_params=pltpu.CompilerParams(
                collective_id=0, has_side_effects=True, vmem_limit_bytes=40 * 1024 * 1024
            ),
            name="conv_lstm",
        )(*operands)
        hidden = pltpu.with_memory_space_constraint(hidden, pltpu.VMEM)
        memory = pltpu.with_memory_space_constraint(memory, pltpu.VMEM)
        return pl.pallas_call(
            finish,
            out_shape=[
                jax.ShapeDtypeStruct((1, steps, rows, cols, chans), bf16),
                jax.ShapeDtypeStruct((1, rows, cols, chans), f32),
            ],
            in_specs=[in_vmem] * 2,
            out_specs=[in_hbm] * 2,
            scratch_shapes=[
                pltpu.VMEM((steps, rows, cols, chans), bf16),
                pltpu.VMEM((rows, cols, chans), f32),
                pltpu.SemaphoreType.DMA((steps + 1,)),
            ],
            compiler_params=pltpu.CompilerParams(vmem_limit_bytes=16 * 1024 * 1024),
            name="write_out",
        )(hidden, memory)

    in_specs = (
        P(None, None, "lon", None),
        P("layer", None, None, None),
        P("layer", None),
        P("layer", None, "lon", None),
        P("layer", None, "lon", None),
    )
    out_specs = (P("layer", None, None, "lon", None), P("layer", None, "lon", None))
    return jax.shard_map(local, mesh=mesh, in_specs=in_specs, out_specs=out_specs, check_vma=False)
```

time: 36.4 us -> 28 us (0.77)
  the two profiles are of different devices: /device:TPU:33 before, /device:TPU:127 now
where the time goes in v2:
time: 28 us; the launch traced here: 27.9 us
  Pallas kernels  27.3 us (98%)
  between operations  0.64 us (2%)
    pallas_call x1, Pallas kernels, local(): pl.pallas_call(lambda *refs: kernel(layers, sectors, *refs), out_shape=[p...  26.2 us
    pallas_call x1, Pallas kernels, local(): pl.pallas_call(finish, out_shape=[jax.ShapeDtypeStruct((1, steps, rows, c...  1.08 us

profile of v2, /device:TPU:127, one launch (start us, length us, event | category | flops | bytes accessed | tf_op | source)
XLA Modules:
  0.0 27.9 jit_solution(2091650337831904122)
XLA Ops:
  0.6 26.2 %conv_lstm.1 = (bf16[2,48,32,128]{3,2,1,0:T(8,128)(2,1)S(1)}, f32[48,32,128]{2,1,0:T(8,128)S(1)}) custom-call(bf16[2,32,32,128]{3,2,1,0:T(8,128)(2,1)} %refs_0_.1, bf16[1,9,256,512]{3,2,1,0:T(8,128)(2,1)} %refs_1_.1, f32[1,512]{1,0:T(1,128)} %refs_2_.1, bf16[1,32,32,128]{3,2,1,0:T(8,128)(2,1)} %refs_3_.1, f32[1,32,32,128]{3,2,1,0:T(8,128)} %refs_4_.1), custom_call_target="tpu_custom_call" | custom-call | tf_op jit(solution)/shard_map/conv_lstm/pallas_call | solution.py:316
  26.8 1.1 %write_out.1 = (bf16[1,2,32,32,128]{4,3,2,1,0:T(8,128)(2,1)}, f32[1,32,32,128]{3,2,1,0:T(8,128)}) custom-call(bf16[2,48,32,128]{3,2,1,0:T(8,128)(2,1)S(1)} %get-tuple-element.4.h_ref, f32[48,32,128]{2,1,0:T(8,128)S(1)} %get-tuple-element.5.cell_ref), custom_call_target="tpu_custom_call" | custom-call | tf_op jit(solution)/shard_map/write_out/pallas_call | solution.py:351

commit v3 on v2

v3 whole, which is shorter than its diff:
```python
import jax
import jax.numpy as jnp
from jax import lax
from jax.experimental import pallas as pl
from jax.experimental.pallas import tpu as pltpu
from jax.sharding import PartitionSpec as P

MESH = pl.DeviceIdType.MESH
PAD = 8
WIDTH = 48
EDGE = 5
ORDER = (
    (0, "mid"), (0, "near"), (1, "mid"), (1, "near"),
    (0, "side"), (1, "side"), (0, "other"), (1, "other"),
)
CHUNKS = ("mid", "near", "side", "other")


def row_shifts(columns):
    blank = jnp.zeros((columns.shape[0], 1, columns.shape[2]), columns.dtype)
    above = jnp.concatenate([blank, columns[:, :-1]], axis=1)
    below = jnp.concatenate([columns[:, 1:], blank], axis=1)
    return above, below


def gate_update(gate_sums, memory):
    chans = memory.shape[-1]
    ingate = 0.5 * jnp.tanh(0.5 * gate_sums[:, :chans]) + 0.5
    forget = 0.5 * jnp.tanh(0.5 * gate_sums[:, chans : 2 * chans]) + 0.5
    candidate = jnp.tanh(gate_sums[:, 2 * chans : 3 * chans])
    outgate = 0.5 * jnp.tanh(0.5 * gate_sums[:, 3 * chans :]) + 0.5
    new_memory = forget * memory + ingate * candidate
    return outgate * jnp.tanh(new_memory), new_memory


def kernel(
    layers, sectors,
    frames, weights, biases, hidden_init, cell_init, h_out, cell_out,
    w, bias, stage_h, stage_c, stage_u, h_old, h_new, hs, uc, us, cell_old, cell_mid, cell_new, partial_mid, partial_near,
    load_sem, w_sem, edge_send, edge_recv, next_send, next_recv, late_sem,
):
    layer, sector = lax.axis_index("layer"), lax.axis_index("lon")
    right, left = lax.rem(sector + 1, sectors), lax.rem(sector + sectors - 1, sectors)
    steps, rows, cols, chans = stage_u.shape
    first, last = sector == 0, sector == sectors - 1
    far = jnp.logical_or(sector == sectors // 2 - 1, sector == sectors // 2)
    h_at = [h_old] + [h_new.at[t] for t in range(steps)]
    cell_at = [cell_old, cell_mid, cell_new]
    base, upper = layer == 0, layer > 0
    flipped = jnp.logical_or(last, sector == sectors // 2 - 1)

    load_h = pltpu.make_async_copy(hidden_init.at[0], stage_h, load_sem.at[0])
    load_c = pltpu.make_async_copy(cell_init.at[0], stage_c, load_sem.at[1])
    load_u = [pltpu.make_async_copy(frames.at[t], stage_u.at[t], load_sem.at[2 + t]) for t in range(steps)]
    load_b = pltpu.make_async_copy(biases, bias, load_sem.at[4])
    load_w = [pltpu.make_async_copy(weights.at[0, i], w.at[i], w_sem.at[i]) for i in range(9)]

    barrier = pltpu.get_barrier_semaphore()
    load_h.start()

    @pl.when(base)
    def _():
        load_u[0].start()

    pl.semaphore_signal(barrier, inc=1, device_id=(layer, left), device_id_type=MESH)

    @pl.when(jnp.logical_not(last))
    def _():
        pl.semaphore_signal(barrier, inc=1, device_id=(layer, right), device_id_type=MESH)

    @pl.when(upper)
    def _():
        pl.semaphore_signal(barrier, inc=1, device_id=(layer - 1, sector), device_id_type=MESH)

    load_c.start()
    for copy in load_w:
        copy.start()
    load_b.start()

    @pl.when(base)
    def _():
        load_u[1].start()

    def edge_copies(index, buffer, width):
        return [
            pltpu.make_async_remote_copy(
                src_ref=buffer.at[pl.ds(source, width)],
                dst_ref=buffer.at[pl.ds(target, width)],
                send_sem=edge_send.at[2 * index + which],
                recv_sem=edge_recv.at[2 * index + which],
                device_id=(layer, side),
                device_id_type=MESH,
            )
            for side, source, target, which in (
                (right, PAD + cols - width, PAD - width, 0),
                (left, PAD, PAD + cols, 1),
            )
        ]

    edges_u = [edge_copies(2 + t, uc.at[t], EDGE - t) for t in range(steps)]

    def edges_of(known):
        return [edge_copies(0, h_old, EDGE - known), edge_copies(1, cell_old, EDGE - 1 - known)]

    def each_layer(act):
        for known in range(layers):

            @pl.when(layer == known)
            def _():
                act(known)

    def place(target, staged, start, stop):
        target[pl.ds(PAD + start, stop - start)] = jnp.swapaxes(staged[:, start:stop], 0, 1)

    def shift_into(center, shifted, start, count):
        above, below = row_shifts(center[pl.ds(start, count)])
        shifted[0, pl.ds(start, count)] = above
        shifted[1, pl.ds(start, count)] = below

    def start_edges(edges):
        edges[0].start()

        @pl.when(jnp.logical_not(first))
        def _():
            edges[1].start()

    def greet():
        awaited = 3 - (layer == layers - 1).astype(jnp.int32) - first.astype(jnp.int32)
        pl.semaphore_wait(barrier, awaited)

        @pl.when(last)
        def _():
            pl.semaphore_signal(late_sem, inc=1, device_id=(layer, right), device_id_type=MESH)

    def send_edges():
        def send(known):
            edges_h, edges_c = edges_of(known)
            start_edges(edges_h)
            if known == 0:
                start_edges(edges_u[0])
            start_edges(edges_c)

        each_layer(send)

    def send_edges_late():
        pl.semaphore_wait(late_sem, 1)

        def send(known):
            edges_h, edges_c = edges_of(known)
            edges_h[1].start()
            if known == 0:
                edges_u[0][1].start()
            edges_c[1].start()
            if known == 0:
                edges_u[1][1].start()

        each_layer(send)

    early = jnp.logical_and(base, last)

    @pl.when(early)
    def _():
        greet()

    load_h.wait()
    place(h_old, stage_h, 0, cols)

    @pl.when(early)
    def _():
        start_edges(edges_of(0)[0])

    @pl.when(base)
    def _():
        load_u[0].wait()
        place(uc.at[0], stage_u.at[0], 0, cols)

    @pl.when(early)
    def _():
        start_edges(edges_u[0])

    load_c.wait()
    place(cell_old, stage_c, 0, cols)

    @pl.when(early)
    def _():
        start_edges(edges_of(0)[1])

    @pl.when(jnp.logical_and(base, jnp.logical_not(jnp.logical_or(last, far))))
    def _():
        greet()
        send_edges()

    shift_into(h_old, hs.at[0], PAD, cols)

    @pl.when(base)
    def _():
        shift_into(uc.at[0], us.at[0], PAD, cols)

    def load_second_input():
        load_u[1].wait()
        place(uc.at[1], stage_u.at[1], 0, cols)
        start_edges(edges_u[1])
        shift_into(uc.at[1], us.at[1], PAD, cols)

    pl.when(early)(load_second_input)

    def finish_edges(which):
        def act(known):
            for edges in edges_of(known):
                edges[which].wait_recv()
            width = EDGE - known
            start = (PAD - width, PAD + cols)[which]
            shift_into(h_old, hs.at[0], start, width)
            if known == 0:
                edges_u[0][which].wait_recv()
                shift_into(uc.at[0], us.at[0], start, width)

        each_layer(act)

    def finish_second_input(which):
        @pl.when(base)
        def _():
            edges_u[1][which].wait_recv()
            shift_into(uc.at[1], us.at[1], (PAD - EDGE + 1, PAD + cols)[which], EDGE - 1)

    def on_side(chunk, act):
        left_now = flipped if chunk == "side" else jnp.logical_not(flipped)

        @pl.when(left_now)
        def _():
            act(0)

        @pl.when(jnp.logical_not(left_now))
        def _():
            act(1)

    def spans(depth, chunk):
        if chunk == "mid":
            return (PAD + 8 + depth,), 16 - 2 * depth
        if chunk == "near":
            return (PAD + 1 + depth, PAD + 24 - depth), 7
        to_left, to_right = PAD - 4 + depth, PAD + 31 - depth
        left_now = flipped if chunk == "side" else jnp.logical_not(flipped)
        return (jnp.where(left_now, to_left, to_right),), 5

    def to_next(t, chunk, pieces):
        return [
            pltpu.make_async_remote_copy(
                src_ref=h_new.at[t, pl.ds(start, count)],
                dst_ref=uc.at[t, pl.ds(start, count)],
                send_sem=next_send.at[t, CHUNKS.index(chunk), i],
                recv_sem=next_recv.at[t, CHUNKS.index(chunk), i],
                device_id=(layer + 1, sector),
                device_id_type=MESH,
            )
            for i, (start, count) in enumerate(pieces)
        ]

    def each_piece(t, chunk, source, act):
        def each(known):
            starts, count = spans(known + t, chunk)
            pieces = tuple((start, count) for start in starts)
            for copy, piece in zip(to_next(t, chunk, pieces), pieces):
                act(copy, piece)

        if chunk == "mid":
            for known in range(layers - 1):
                pl.when(source == known)(lambda known=known: each(known))
        else:
            pl.when(jnp.logical_and(source >= 0, source < layers - 1))(lambda: each(source))

    def receive(t, chunk):
        def act(copy, piece):
            copy.wait_recv()
            shift_into(uc.at[t], us.at[t], *piece)

        each_piece(t, chunk, layer - 1, act)

    def windows(center, shifted, starts, count):
        pick = (lambda s: shifted[0, s], lambda s: center[s], lambda s: shifted[1, s])
        return [
            jnp.concatenate([pick[a](pl.ds(start + b - 1, count)).reshape(-1, chans) for start in starts], axis=0)
            for a in range(3)
            for b in range(3)
        ]

    def product(parts, filters):
        return jnp.dot(
            jnp.concatenate(parts, axis=1), filters.reshape(-1, 4 * chans), preferred_element_type=jnp.float32
        )

    def update(t, starts, count, sums):
        memory = jnp.concatenate([cell_at[t][pl.ds(start, count)].reshape(-1, chans) for start in starts], axis=0)
        hidden, memory = gate_update(sums, memory)
        hidden = hidden.astype(jnp.bfloat16).reshape(len(starts), count, rows, chans)
        memory = memory.reshape(len(starts), count, rows, chans)
        for i, start in enumerate(starts):
            h_new[t, pl.ds(start, count)] = hidden[i]
            cell_at[t + 1][pl.ds(start, count)] = memory[i]
        if t + 1 < steps:
            for i, start in enumerate(starts):
                above, below = row_shifts(hidden[i])
                hs[t + 1, 0, pl.ds(start, count)] = above
                hs[t + 1, 1, pl.ds(start, count)] = below

    partial = {"mid": partial_mid, "near": partial_near}

    def by_layer(chunk, act):
        if chunk == "mid":
            for known in range(layers):
                pl.when(layer == known)(lambda known=known: act(known > 0, known))
        else:
            pl.when(base)(lambda: act(False, 0))
            pl.when(upper)(lambda: act(True, layer))

    def prepare(t, chunk):
        def act(above_first, own):
            if above_first:
                starts, count = spans(own + t, chunk)
                sums = product(windows(h_at[t], hs.at[t], starts, count), w[:, chans:]) + bias[...]
                partial[chunk][pl.ds(0, sums.shape[0])] = sums

        by_layer(chunk, act)

    def compute(t, chunk):
        def whole(own):
            starts, count = spans(own + t, chunk)
            pairs = zip(windows(uc.at[t], us.at[t], starts, count), windows(h_at[t], hs.at[t], starts, count))
            update(t, starts, count, product([part for pair in pairs for part in pair], w[...]) + bias[...])

        def act(above_first, own):
            if above_first:
                starts, count = spans(own + t, chunk)
                sums = product(windows(uc.at[t], us.at[t], starts, count), w[:, :chans])
                update(t, starts, count, sums + partial[chunk][pl.ds(0, sums.shape[0])])
            else:
                whole(own)

        if chunk in partial:
            by_layer(chunk, act)
        else:
            whole(layer)

    def write_columns(t, start, stop):
        h_out[t, :, start:stop] = jnp.swapaxes(h_new[t, PAD + start : PAD + stop], 0, 1)
        if t == steps - 1:
            cell_out[:, start:stop] = jnp.swapaxes(cell_new[PAD + start : PAD + stop], 0, 1)

    for copy in load_w:
        copy.wait()
    load_b.wait()

    @pl.when(upper)
    def _():
        prepare(0, "mid")
        prepare(0, "near")
        greet()
        send_edges()

    for t, chunk in ORDER:
        if (t, chunk) == (0, "side"):
            pl.when(jnp.logical_and(first, base))(send_edges_late)
        if (t, chunk) == (0, "other"):

            @pl.when(upper)
            def _():
                for s in range(steps):
                    write_columns(s, 8, cols - 8)

        if chunk in ("side", "other"):
            on_side(chunk, finish_second_input if t else finish_edges)
        receive(t, chunk)
        compute(t, chunk)
        if (t, chunk) == (0, "mid"):

            @pl.when(jnp.logical_and(base, far))
            def _():
                greet()
                send_edges()

        each_piece(t, chunk, layer, lambda copy, piece: copy.start())
        if (t, chunk) == (0, "mid"):
            pl.when(jnp.logical_and(base, jnp.logical_not(last)))(load_second_input)
            prepare(1, "mid")
        if (t, chunk) == (0, "near"):

            @pl.when(upper)
            def _():
                pl.when(first)(send_edges_late)
                prepare(1, "near")

    for t in range(steps):
        write_columns(t, 0, 8)
        write_columns(t, cols - 8, cols)

    @pl.when(base)
    def _():
        for t in range(steps):
            write_columns(t, 8, cols - 8)

    def sent(known):
        for edges in edges_of(known) + (edges_u if known == 0 else []):
            for copy in edges:
                copy.wait_send()

    each_layer(sent)
    for t, chunk in ORDER:
        each_piece(t, chunk, layer, lambda copy, piece: copy.wait_send())


def finish(h_ref, cell_ref, hidden_out, cell_out, sems):
    copies = [pltpu.make_async_copy(h_ref.at[t], hidden_out.at[0, t], sems.at[t]) for t in range(h_ref.shape[0])]
    copies.append(pltpu.make_async_copy(cell_ref, cell_out.at[0], sems.at[h_ref.shape[0]]))
    for copy in copies:
        copy.start()
    for copy in copies:
        copy.wait()


def solution(mesh):
    layers, sectors = mesh.shape["layer"], mesh.shape["lon"]

    def local(frames, weights, biases, hidden_init, cell_init):
        steps, rows, cols, chans = frames.shape
        bf16, f32 = jnp.bfloat16, jnp.float32
        in_hbm = pl.BlockSpec(memory_space=pltpu.HBM)
        in_vmem = pl.BlockSpec(memory_space=pltpu.VMEM)
        operands = [
            pltpu.with_memory_space_constraint(x, pltpu.HBM)
            for x in (frames, weights, biases, hidden_init, cell_init)
        ]
        hidden, memory = pl.pallas_call(
            lambda *refs: kernel(layers, sectors, *refs),
            out_shape=[
                pltpu.VMEM((steps, rows, cols, chans), bf16),
                pltpu.VMEM((rows, cols, chans), f32),
            ],
            in_specs=[in_hbm] * 5,
            out_specs=[in_vmem] * 2,
            scratch_shapes=[
                pltpu.VMEM((9, 2 * chans, 4 * chans), bf16),
                pltpu.VMEM((1, 4 * chans), f32),
                pltpu.VMEM((rows, cols, chans), bf16),
                pltpu.VMEM((rows, cols, chans), f32),
                pltpu.VMEM((steps, rows, cols, chans), bf16),
                pltpu.VMEM((WIDTH, rows, chans), bf16),
                pltpu.VMEM((steps, WIDTH, rows, chans), bf16),
                pltpu.VMEM((steps, 2, WIDTH, rows, chans), bf16),
                pltpu.VMEM((steps, WIDTH, rows, chans), bf16),
                pltpu.VMEM((steps, 2, WIDTH, rows, chans), bf16),
                pltpu.VMEM((WIDTH, rows, chans), f32),
                pltpu.VMEM((WIDTH, rows, chans), f32),
                pltpu.VMEM((WIDTH, rows, chans), f32),
                pltpu.VMEM((16 * rows, 4 * chans), f32),
                pltpu.VMEM((14 * rows, 4 * chans), f32),
                pltpu.SemaphoreType.DMA((5,)),
                pltpu.SemaphoreType.DMA((9,)),
                pltpu.SemaphoreType.DMA((8,)),
                pltpu.SemaphoreType.DMA((8,)),
                pltpu.SemaphoreType.DMA((steps, 4, 2)),
                pltpu.SemaphoreType.DMA((steps, 4, 2)),
                pltpu.SemaphoreType.REGULAR,
            ],
            compiler_params=pltpu.CompilerParams(
                collective_id=0, has_side_effects=True, vmem_limit_bytes=40 * 1024 * 1024
            ),
            name="conv_lstm",
        )(*operands)
        hidden = pltpu.with_memory_space_constraint(hidden, pltpu.VMEM)
        memory = pltpu.with_memory_space_constraint(memory, pltpu.VMEM)
        return pl.pallas_call(
            finish,
            out_shape=[
                jax.ShapeDtypeStruct((1, steps, rows, cols, chans), bf16),
                jax.ShapeDtypeStruct((1, rows, cols, chans), f32),
            ],
            in_specs=[in_vmem] * 2,
            out_specs=[in_hbm] * 2,
            scratch_shapes=[pltpu.SemaphoreType.DMA((steps + 1,))],
            compiler_params=pltpu.CompilerParams(vmem_limit_bytes=16 * 1024 * 1024),
            name="write_out",
        )(hidden, memory)

    in_specs = (
        P(None, None, "lon", None),
        P("layer", None, None, None),
        P("layer", None),
        P("layer", None, "lon", None),
        P("layer", None, "lon", None),
    )
    out_specs = (P("layer", None, None, "lon", None), P("layer", None, "lon", None))
    return jax.shard_map(local, mesh=mesh, in_specs=in_specs, out_specs=out_specs, check_vma=False)
```

time: 28 us -> 24.7 us (0.88)
  the two profiles are of different devices: /device:TPU:127 before, /device:TPU:33 now
where the time goes in v3:
time: 24.7 us; the launch traced here: 24.5 us
  Pallas kernels  23.9 us (97%)
  between operations  0.64 us (3%)
    pallas_call x1, Pallas kernels, local(): pl.pallas_call(lambda *refs: kernel(layers, sectors, *refs), out_shape=[p...  22.9 us
    pallas_call x1, Pallas kernels, local(): pl.pallas_call(finish, out_shape=[jax.ShapeDtypeStruct((1, steps, rows, c...  0.99 us

profile of v3, /device:TPU:33, one launch (start us, length us, event | category | flops | bytes accessed | tf_op | source)
XLA Modules:
  0.0 24.5 jit_solution(3619608578931313647)
XLA Ops:
  0.6 22.9 %conv_lstm.1 = (bf16[2,32,32,128]{3,2,1,0:T(8,128)(2,1)S(1)}, f32[32,32,128]{2,1,0:T(8,128)S(1)}) custom-call(bf16[2,32,32,128]{3,2,1,0:T(8,128)(2,1)} %refs_0_.1, bf16[1,9,256,512]{3,2,1,0:T(8,128)(2,1)} %refs_1_.1, f32[1,512]{1,0:T(1,128)} %refs_2_.1, bf16[1,32,32,128]{3,2,1,0:T(8,128)(2,1)} %refs_3_.1, f32[1,32,32,128]{3,2,1,0:T(8,128)} %refs_4_.1), custom_call_target="tpu_custom_call" | custom-call | tf_op jit(solution)/shard_map/conv_lstm/pallas_call | solution.py:432
  23.5 1.0 %write_out.1 = (bf16[1,2,32,32,128]{4,3,2,1,0:T(8,128)(2,1)}, f32[1,32,32,128]{3,2,1,0:T(8,128)}) custom-call(bf16[2,32,32,128]{3,2,1,0:T(8,128)(2,1)S(1)} %get-tuple-element.4.h_ref, f32[32,32,128]{2,1,0:T(8,128)S(1)} %get-tuple-element.5.cell_ref), custom_call_target="tpu_custom_call" | custom-call | tf_op jit(solution)/shard_map/write_out/pallas_call | solution.py:471

commit v4 on v3

v4 whole, which is shorter than its diff:
```python
import jax
import jax.numpy as jnp
from jax import lax
from jax.experimental import pallas as pl
from jax.experimental.pallas import tpu as pltpu
from jax.sharding import PartitionSpec as P

MESH = pl.DeviceIdType.MESH
PAD = 8
WIDTH = 48
EDGE = 5
BLOCKS = (
    ((0, "mid"),), ((0, "near"),), ((1, "mid"),), ((1, "near"),), ((0, "side"),), ((1, "side"),), ((0, "other"),), ((1, "other"),),
)
CHUNKS = ("mid", "near", "side", "other")


def row_shifts(columns):
    blank = jnp.zeros((columns.shape[0], 1, columns.shape[2]), columns.dtype)
    above = jnp.concatenate([blank, columns[:, :-1]], axis=1)
    below = jnp.concatenate([columns[:, 1:], blank], axis=1)
    return above, below


def gate_update(gate_sums, memory):
    chans = memory.shape[-1]
    ingate = 0.5 * jnp.tanh(0.5 * gate_sums[:, :chans]) + 0.5
    forget = 0.5 * jnp.tanh(0.5 * gate_sums[:, chans : 2 * chans]) + 0.5
    candidate = jnp.tanh(gate_sums[:, 2 * chans : 3 * chans])
    outgate = 0.5 * jnp.tanh(0.5 * gate_sums[:, 3 * chans :]) + 0.5
    new_memory = forget * memory + ingate * candidate
    return outgate * jnp.tanh(new_memory), new_memory


def kernel(layers, sectors, *refs):
    for layer in range(layers):
        pl.when(lax.axis_index("layer") == layer)(lambda layer=layer: layer_program(layer, layers, sectors, *refs))


def layer_program(
    layer, layers, sectors,
    frames, weights, biases, hidden_init, cell_init, h_out, cell_out,
    w, bias, stage_h, stage_c, stage_u, h_old, h_new, hs, uc, us, cell_old, cell_edge, cell_mid, cell_new,
    partial_mid, partial_near, load_sem, w_sem, edge_send, edge_recv, next_send, next_recv, late_sem,
):
    sector = lax.axis_index("lon")
    right, left = lax.rem(sector + 1, sectors), lax.rem(sector + sectors - 1, sectors)
    steps, rows, cols, chans = stage_u.shape
    base, top = layer == 0, layer == layers - 1
    first, last = sector == 0, sector == sectors - 1
    far_or_last = jnp.logical_or(jnp.logical_or(sector == sectors // 2 - 1, sector == sectors // 2), last)
    flipped = lax.rem(sector, 4) == 3
    h_at = [h_old] + [h_new.at[t] for t in range(steps)]
    cell_at = [cell_old, cell_mid, cell_new]
    partial = {"mid": partial_mid, "near": partial_near}

    load_h = pltpu.make_async_copy(hidden_init.at[0], stage_h, load_sem.at[0])
    load_c = pltpu.make_async_copy(cell_init.at[0], stage_c, load_sem.at[1])
    load_u = [pltpu.make_async_copy(frames.at[t], stage_u.at[t], load_sem.at[2 + t]) for t in range(steps)]
    load_b = pltpu.make_async_copy(biases, bias, load_sem.at[4])
    load_w = [pltpu.make_async_copy(weights.at[0, i], w.at[i], w_sem.at[i]) for i in range(9)]

    barrier = pltpu.get_barrier_semaphore()
    load_h.start()
    if base:
        load_u[0].start()
    pl.semaphore_signal(barrier, inc=1, device_id=(layer, left), device_id_type=MESH)

    @pl.when(jnp.logical_not(last))
    def _():
        pl.semaphore_signal(barrier, inc=1, device_id=(layer, right), device_id_type=MESH)

    if not base:
        pl.semaphore_signal(barrier, inc=1, device_id=(layer - 1, sector), device_id_type=MESH)
    load_c.start()
    for copy in load_w:
        copy.start()
    load_b.start()
    if base:
        load_u[1].start()

    def edge_copies(index, buffer, width):
        return [
            pltpu.make_async_remote_copy(
                src_ref=buffer.at[pl.ds(source, width)],
                dst_ref=buffer.at[pl.ds(target, width)],
                send_sem=edge_send.at[2 * index + which],
                recv_sem=edge_recv.at[2 * index + which],
                device_id=(layer, side),
                device_id_type=MESH,
            )
            for side, source, target, which in (
                (right, PAD + cols - width, PAD - width, 0),
                (left, PAD, PAD + cols, 1),
            )
        ]

    width = EDGE - layer
    edges_h = edge_copies(0, h_old, width)
    edges_c = edge_copies(1, cell_edge, width - 1)
    edges_u = [edge_copies(2 + t, uc.at[t], width - t) for t in range(steps)] if base else []
    soon = [edges_h] + edges_u[:1] + [edges_c]

    def place(target, staged, start, stop):
        target[pl.ds(PAD + start, stop - start)] = jnp.swapaxes(staged[:, start:stop], 0, 1)

    def shift_into(center, shifted, start, count):
        above, below = row_shifts(center[pl.ds(start, count)])
        shifted[0, pl.ds(start, count)] = above
        shifted[1, pl.ds(start, count)] = below

    def start_edges(groups):
        for edges in groups:
            edges[0].start()

        @pl.when(jnp.logical_not(first))
        def _():
            for edges in groups:
                edges[1].start()

    def start_edges_late():
        pl.semaphore_wait(late_sem, 1)
        for edges in soon + edges_u[1:]:
            edges[1].start()

    def greet():
        pl.semaphore_wait(barrier, (2 if top else 3) - first.astype(jnp.int32))

    @pl.when(last)
    def _():
        greet()
        pl.semaphore_signal(late_sem, inc=1, device_id=(layer, right), device_id_type=MESH)

    load_h.wait()
    place(h_old, stage_h, 0, cols)
    if base:
        pl.when(last)(lambda: start_edges([edges_h]))
        load_u[0].wait()
        place(uc.at[0], stage_u.at[0], 0, cols)
        pl.when(last)(lambda: start_edges([edges_u[0]]))
    shift_into(h_old, hs.at[0], PAD, cols)
    if base:
        shift_into(uc.at[0], us.at[0], PAD, cols)
    load_c.wait()
    place(cell_old, stage_c, 0, cols)
    for start in (PAD, PAD + cols - EDGE + 1):
        cell_edge[pl.ds(start, EDGE - 1)] = cell_old[pl.ds(start, EDGE - 1)].astype(jnp.bfloat16)
    if base:
        pl.when(last)(lambda: start_edges([edges_c]))

    def load_second_input():
        load_u[1].wait()
        place(uc.at[1], stage_u.at[1], 0, cols)
        start_edges([edges_u[1]])
        shift_into(uc.at[1], us.at[1], PAD, cols)

    def finish_edges(which):
        edges_h[which].wait_recv()
        edges_c[which].wait_recv()
        start = (PAD - width, PAD + cols)[which]
        shift_into(h_old, hs.at[0], start, width)
        edge = pl.ds((PAD - width + 1, PAD + cols)[which], width - 1)
        cell_old[edge] = cell_edge[edge].astype(jnp.float32)
        if base:
            edges_u[0][which].wait_recv()
            shift_into(uc.at[0], us.at[0], start, width)

    def finish_second_input(which):
        edges_u[1][which].wait_recv()
        shift_into(uc.at[1], us.at[1], (PAD - EDGE + 1, PAD + cols)[which], EDGE - 1)

    def is_left(chunk):
        return flipped if chunk == "side" else jnp.logical_not(flipped)

    def on_side(chunk, act):
        pl.when(is_left(chunk))(lambda: act(0))
        pl.when(jnp.logical_not(is_left(chunk)))(lambda: act(1))

    def spans(depth, chunk):
        if chunk == "mid":
            return (PAD + 8 + depth,), 16 - 2 * depth
        if chunk == "near":
            return (PAD + 1 + depth, PAD + 24 - depth), 7
        return (jnp.where(is_left(chunk), PAD - 4 + depth, PAD + 31 - depth),), 5

    def to_next(t, chunk, source):
        starts, count = spans(source + t, chunk)
        return [
            (
                pltpu.make_async_remote_copy(
                    src_ref=h_new.at[t, pl.ds(start, count)],
                    dst_ref=uc.at[t, pl.ds(start, count)],
                    send_sem=next_send.at[t, CHUNKS.index(chunk), i],
                    recv_sem=next_recv.at[t, CHUNKS.index(chunk), i],
                    device_id=(source + 1, sector),
                    device_id_type=MESH,
                ),
                start,
                count,
            )
            for i, start in enumerate(starts)
        ]

    def windows(center, shifted, starts, count):
        pick = (lambda s: shifted[0, s], lambda s: center[s], lambda s: shifted[1, s])
        return [
            jnp.concatenate([pick[a](pl.ds(start + b - 1, count)).reshape(-1, chans) for start in starts], axis=0)
            for a in range(3)
            for b in range(3)
        ]

    def product(parts, filters):
        return jnp.dot(
            jnp.concatenate(parts, axis=1), filters.reshape(-1, 4 * chans), preferred_element_type=jnp.float32
        )

    def prepare(t, chunk):
        starts, count = spans(layer + t, chunk)
        sums = product(windows(h_at[t], hs.at[t], starts, count), w[:, chans:]) + bias[...]
        partial[chunk][pl.ds(0, sums.shape[0])] = sums

    def compute(t, chunk):
        starts, count = spans(layer + t, chunk)
        inputs = windows(uc.at[t], us.at[t], starts, count)
        if chunk in partial and not base:
            sums = product(inputs, w[:, :chans])
            sums = sums + partial[chunk][pl.ds(0, sums.shape[0])]
        else:
            pairs = zip(inputs, windows(h_at[t], hs.at[t], starts, count))
            sums = product([part for pair in pairs for part in pair], w[...]) + bias[...]
        memory = jnp.concatenate([cell_at[t][pl.ds(start, count)].reshape(-1, chans) for start in starts], axis=0)
        hidden, memory = gate_update(sums, memory)
        hidden = hidden.astype(jnp.bfloat16).reshape(len(starts), count, rows, chans)
        memory = memory.reshape(len(starts), count, rows, chans)
        for i, start in enumerate(starts):
            h_new[t, pl.ds(start, count)] = hidden[i]
            cell_at[t + 1][pl.ds(start, count)] = memory[i]
        if t + 1 < steps:
            for i, start in enumerate(starts):
                above, below = row_shifts(hidden[i])
                hs[t + 1, 0, pl.ds(start, count)] = above
                hs[t + 1, 1, pl.ds(start, count)] = below

    def write_columns(t, start, stop):
        h_out[t, :, start:stop] = jnp.swapaxes(h_new[t, PAD + start : PAD + stop], 0, 1)
        if t == steps - 1:
            cell_out[:, start:stop] = jnp.swapaxes(cell_new[PAD + start : PAD + stop], 0, 1)

    for copy in load_w:
        copy.wait()
    load_b.wait()
    if not base:
        prepare(0, "mid")
        prepare(0, "near")
        pl.when(jnp.logical_not(last))(greet)
        if layer == 1:
            pl.when(far_or_last)(lambda: start_edges(soon))
        else:
            start_edges(soon)

    for block in BLOCKS:
        if (0, "side") in block:
            if base:
                pl.when(first)(start_edges_late)
            on_side("side", finish_edges)
        if (0, "other") in block:
            on_side("other", finish_edges)
        if (1, "side") in block and base:
            on_side("side", finish_second_input)
        if (1, "other") in block:
            if base:
                on_side("other", finish_second_input)
            else:
                for t in range(steps):
                    write_columns(t, 8, cols - 8)
        if not base:
            arrivals = [(t, *item) for t, chunk in block for item in to_next(t, chunk, layer - 1)]
            for _, copy, _, _ in arrivals:
                copy.wait_recv()
            for t, _, start, count in arrivals:
                shift_into(uc.at[t], us.at[t], start, count)
        for t, chunk in block:
            compute(t, chunk)
        if base and block == BLOCKS[0]:

            @pl.when(jnp.logical_not(last))
            def _():
                greet()
                start_edges(soon)

        if not top:
            for t, chunk in block:
                for copy, _, _ in to_next(t, chunk, layer):
                    copy.start()
        if block == BLOCKS[0]:
            if base:
                load_second_input()
            else:
                if layer == 1:
                    pl.when(jnp.logical_not(far_or_last))(lambda: start_edges(soon))
                prepare(1, "mid")
        if block == BLOCKS[1] and not base:
            prepare(1, "near")
        if block == BLOCKS[2] and not base:
            pl.when(first)(start_edges_late)

    for t in range(steps):
        write_columns(t, 0, 8)
        write_columns(t, cols - 8, cols)
    if base:
        for t in range(steps):
            write_columns(t, 8, cols - 8)

    for edges in soon + edges_u[1:]:
        for copy in edges:
            copy.wait_send()
    if not top:
        for block in BLOCKS:
            for t, chunk in block:
                for copy, _, _ in to_next(t, chunk, layer):
                    copy.wait_send()


def finish(h_ref, cell_ref, hidden_out, cell_out, sems):
    steps, rows = h_ref.shape[:2]
    half = rows // 2
    copies = []
    for start in (0, half):
        part = pl.ds(start, half)
        pairs = [(h_ref.at[t, part], hidden_out.at[0, t, part]) for t in range(steps)]
        for source, target in pairs + [(cell_ref.at[part], cell_out.at[0, part])]:
            copies.append(pltpu.make_async_copy(source, target, sems.at[len(copies)]))
            copies[-1].start()
    for copy in copies:
        copy.wait()


def solution(mesh):
    layers, sectors = mesh.shape["layer"], mesh.shape["lon"]

    def local(frames, weights, biases, hidden_init, cell_init):
        steps, rows, cols, chans = frames.shape
        bf16, f32 = jnp.bfloat16, jnp.float32
        in_hbm = pl.BlockSpec(memory_space=pltpu.HBM)
        in_vmem = pl.BlockSpec(memory_space=pltpu.VMEM)
        operands = [
            pltpu.with_memory_space_constraint(x, pltpu.HBM)
            for x in (frames, weights, biases, hidden_init, cell_init)
        ]
        hidden, memory = pl.pallas_call(
            lambda *refs: kernel(layers, sectors, *refs),
            out_shape=[
                pltpu.VMEM((steps, rows, cols, chans), bf16),
                pltpu.VMEM((rows, cols, chans), f32),
            ],
            in_specs=[in_hbm] * 5,
            out_specs=[in_vmem] * 2,
            scratch_shapes=[
                pltpu.VMEM((9, 2 * chans, 4 * chans), bf16),
                pltpu.VMEM((1, 4 * chans), f32),
                pltpu.VMEM((rows, cols, chans), bf16),
                pltpu.VMEM((rows, cols, chans), f32),
                pltpu.VMEM((steps, rows, cols, chans), bf16),
                pltpu.VMEM((WIDTH, rows, chans), bf16),
                pltpu.VMEM((steps, WIDTH, rows, chans), bf16),
                pltpu.VMEM((steps, 2, WIDTH, rows, chans), bf16),
                pltpu.VMEM((steps, WIDTH, rows, chans), bf16),
                pltpu.VMEM((steps, 2, WIDTH, rows, chans), bf16),
                pltpu.VMEM((WIDTH, rows, chans), f32),
                pltpu.VMEM((WIDTH, rows, chans), bf16),
                pltpu.VMEM((WIDTH, rows, chans), f32),
                pltpu.VMEM((WIDTH, rows, chans), f32),
                pltpu.VMEM((16 * rows, 4 * chans), f32),
                pltpu.VMEM((14 * rows, 4 * chans), f32),
                pltpu.SemaphoreType.DMA((5,)),
                pltpu.SemaphoreType.DMA((9,)),
                pltpu.SemaphoreType.DMA((8,)),
                pltpu.SemaphoreType.DMA((8,)),
                pltpu.SemaphoreType.DMA((steps, 4, 2)),
                pltpu.SemaphoreType.DMA((steps, 4, 2)),
                pltpu.SemaphoreType.REGULAR,
            ],
            compiler_params=pltpu.CompilerParams(
                collective_id=0, has_side_effects=True, vmem_limit_bytes=40 * 1024 * 1024
            ),
            name="conv_lstm",
        )(*operands)
        hidden = pltpu.with_memory_space_constraint(hidden, pltpu.VMEM)
        memory = pltpu.with_memory_space_constraint(memory, pltpu.VMEM)
        return pl.pallas_call(
            finish,
            out_shape=[
                jax.ShapeDtypeStruct((1, steps, rows, cols, chans), bf16),
                jax.ShapeDtypeStruct((1, rows, cols, chans), f32),
            ],
            in_specs=[in_vmem] * 2,
            out_specs=[in_hbm] * 2,
            scratch_shapes=[pltpu.SemaphoreType.DMA((2 * steps + 2,))],
            compiler_params=pltpu.CompilerParams(vmem_limit_bytes=16 * 1024 * 1024),
            name="write_out",
        )(hidden, memory)

    in_specs = (
        P(None, None, "lon", None),
        P("layer", None, None, None),
        P("layer", None),
        P("layer", None, "lon", None),
        P("layer", None, "lon", None),
    )
    out_specs = (P("layer", None, None, "lon", None), P("layer", None, "lon", None))
    return jax.shard_map(local, mesh=mesh, in_specs=in_specs, out_specs=out_specs, check_vma=False)
```

time: 24.7 us -> 23.2 us (0.939)
  Pallas kernels: 23.9 us -> 22.3 us
    pallas_call x1, Pallas kernels: 22.9 us -> 21.3 us  [local(): pl.pallas_call(lambda *refs: kernel(layers, sectors, *refs), out_shape=[p...]
where the time goes in v4:
time: 23.2 us; the launch traced here: 23.1 us
  Pallas kernels  22.3 us (96%)
  between operations  0.8 us (3%)
    pallas_call x1, Pallas kernels, local(): pl.pallas_call(lambda *refs: kernel(layers, sectors, *refs), out_shape=[p...  21.3 us
    pallas_call x1, Pallas kernels, local(): pl.pallas_call(finish, out_shape=[jax.ShapeDtypeStruct((1, steps, rows, c...  1.02 us

profile of v4, /device:TPU:33, one launch (start us, length us, event | category | flops | bytes accessed | tf_op | source)
XLA Modules:
  0.0 23.1 jit_solution(7479532600610118181)
XLA Ops:
  0.6 21.3 %conv_lstm.1 = (bf16[2,32,32,128]{3,2,1,0:T(8,128)(2,1)S(1)}, f32[32,32,128]{2,1,0:T(8,128)S(1)}) custom-call(bf16[2,32,32,128]{3,2,1,0:T(8,128)(2,1)} %refs_0_.1, bf16[1,9,256,512]{3,2,1,0:T(8,128)(2,1)} %refs_1_.1, f32[1,512]{1,0:T(1,128)} %refs_2_.1, bf16[1,32,32,128]{3,2,1,0:T(8,128)(2,1)} %refs_3_.1, f32[1,32,32,128]{3,2,1,0:T(8,128)} %refs_4_.1), custom_call_target="tpu_custom_call" | custom-call | tf_op jit(solution)/shard_map/conv_lstm/pallas_call | solution.py:350
  21.9 1.0 %write_out.1 = (bf16[1,2,32,32,128]{4,3,2,1,0:T(8,128)(2,1)}, f32[1,32,32,128]{3,2,1,0:T(8,128)}) custom-call(bf16[2,32,32,128]{3,2,1,0:T(8,128)(2,1)S(1)} %get-tuple-element.4.h_ref, f32[32,32,128]{2,1,0:T(8,128)S(1)} %get-tuple-element.5.cell_ref), custom_call_target="tpu_custom_call" | custom-call | tf_op jit(solution)/shard_map/write_out/pallas_call | solution.py:390

commit v5 on v4

--- a/solution.py
+++ b/solution.py
@@ -40,15 +40,18 @@
 def layer_program(
     layer, layers, sectors,
     frames, weights, biases, hidden_init, cell_init, h_out, cell_out,
-    w, bias, stage_h, stage_c, stage_u, h_old, h_new, hs, uc, us, cell_old, cell_edge, cell_mid, cell_new,
-    partial_mid, partial_near, load_sem, w_sem, edge_send, edge_recv, next_send, next_recv, late_sem,
+    w, bias, stage_h, stage_c, stage_u, u_far, h_old, h_new, hs, uc, us, cell_old, cell_edge, cell_mid, cell_new,
+    partial_mid, partial_near, load_sem, edge_send, edge_recv, next_send, next_recv, late_sem,
 ):
     sector = lax.axis_index("lon")
     right, left = lax.rem(sector + 1, sectors), lax.rem(sector + sectors - 1, sectors)
     steps, rows, cols, chans = stage_u.shape
     base, top = layer == 0, layer == layers - 1
     first, last = sector == 0, sector == sectors - 1
-    far_or_last = jnp.logical_or(jnp.logical_or(sector == sectors // 2 - 1, sector == sectors // 2), last)
+    far_right = jnp.logical_or(sector == sectors // 2 - 1, last)
+    far_left = jnp.logical_or(sector == sectors // 2, first)
+    far = jnp.logical_or(far_right, far_left)
+    far_or_last = jnp.logical_and(far, jnp.logical_not(first))
     flipped = lax.rem(sector, 4) == 3
     h_at = [h_old] + [h_new.at[t] for t in range(steps)]
     cell_at = [cell_old, cell_mid, cell_new]
@@ -58,7 +61,7 @@
     load_c = pltpu.make_async_copy(cell_init.at[0], stage_c, load_sem.at[1])
     load_u = [pltpu.make_async_copy(frames.at[t], stage_u.at[t], load_sem.at[2 + t]) for t in range(steps)]
     load_b = pltpu.make_async_copy(biases, bias, load_sem.at[4])
-    load_w = [pltpu.make_async_copy(weights.at[0, i], w.at[i], w_sem.at[i]) for i in range(9)]
+    load_w = [pltpu.make_async_copy(weights.at[0, i], w.at[i], load_sem.at[5]) for i in range(9)]
 
     barrier = pltpu.get_barrier_semaphore()
     load_h.start()
@@ -72,19 +75,35 @@
 
     if not base:
         pl.semaphore_signal(barrier, inc=1, device_id=(layer - 1, sector), device_id_type=MESH)
+    else:
+        @pl.when(far)
+        def _():
+            pl.semaphore_signal(barrier, inc=1, device_id=(layers - 1, sectors - 1 - sector), device_id_type=MESH)
+
+    if top:
+
+        @pl.when(far)
+        def _():
+            for copy in load_u:
+                copy.start()
+
     load_c.start()
     for copy in load_w:
         copy.start()
     load_b.start()
     if base:
         load_u[1].start()
+
+    def wait_columns(sem, count):
+        pair = hs.at[0, :, pl.ds(0, count // 2)] if count % 2 == 0 else hs.at[0, 0, pl.ds(0, count)]
+        pltpu.make_async_copy(pair, pair, sem).wait()
 
     def edge_copies(index, buffer, width):
         return [
             pltpu.make_async_remote_copy(
                 src_ref=buffer.at[pl.ds(source, width)],
                 dst_ref=buffer.at[pl.ds(target, width)],
-                send_sem=edge_send.at[2 * index + which],
+                send_sem=edge_send,
                 recv_sem=edge_recv.at[2 * index + which],
                 device_id=(layer, side),
                 device_id_type=MESH,
@@ -97,9 +116,9 @@
 
     width = EDGE - layer
     edges_h = edge_copies(0, h_old, width)
-    edges_c = edge_copies(1, cell_edge, width - 1)
-    edges_u = [edge_copies(2 + t, uc.at[t], width - t) for t in range(steps)] if base else []
-    soon = [edges_h] + edges_u[:1] + [edges_c]
+    edges_c = edge_copies(0, cell_edge, width - 1)
+    edges_u = [edge_copies(t, uc.at[t], width - t) for t in range(steps)] if base else []
+    soon = [edges_h, edges_c]
 
     def place(target, staged, start, stop):
         target[pl.ds(PAD + start, stop - start)] = jnp.swapaxes(staged[:, start:stop], 0, 1)
@@ -118,18 +137,47 @@
             for edges in groups:
                 edges[1].start()
 
+    def start_inputs(t):
+        pl.when(jnp.logical_not(far_right))(edges_u[t][0].start)
+        pl.when(jnp.logical_not(far_left))(edges_u[t][1].start)
+
     def start_edges_late():
         pl.semaphore_wait(late_sem, 1)
-        for edges in soon + edges_u[1:]:
+        for edges in soon:
             edges[1].start()
 
+    def start_far_inputs():
+        for copy in load_u:
+            copy.wait()
+        for which, chosen, source in ((0, far_right, cols - 8), (1, far_left, 0)):
+
+            @pl.when(chosen)
+            def _():
+                for t in range(steps):
+                    u_far[t] = jnp.swapaxes(stage_u[t, :, source : source + 8], 0, 1)
+                for t in range(steps):
+                    count = EDGE - t
+                    pltpu.make_async_remote_copy(
+                        src_ref=u_far.at[t, pl.ds((8 - count, 0)[which], count)],
+                        dst_ref=uc.at[t, pl.ds((PAD - count, PAD + cols)[which], count)],
+                        send_sem=edge_send,
+                        recv_sem=edge_recv.at[2 * t + which],
+                        device_id=(0, sectors - 1 - sector),
+                        device_id_type=MESH,
+                    ).start()
+
     def greet():
-        pl.semaphore_wait(barrier, (2 if top else 3) - first.astype(jnp.int32))
+        awaited = 3 - first.astype(jnp.int32)
+        if top:
+            awaited = awaited - 1 + far.astype(jnp.int32)
+        pl.semaphore_wait(barrier, awaited)
 
     @pl.when(last)
     def _():
         greet()
         pl.semaphore_signal(late_sem, inc=1, device_id=(layer, right), device_id_type=MESH)
+        if top:
+            start_far_inputs()
 
     load_h.wait()
     place(h_old, stage_h, 0, cols)
@@ -137,7 +185,7 @@
         pl.when(last)(lambda: start_edges([edges_h]))
         load_u[0].wait()
         place(uc.at[0], stage_u.at[0], 0, cols)
-        pl.when(last)(lambda: start_edges([edges_u[0]]))
+        pl.when(last)(lambda: start_inputs(0))
     shift_into(h_old, hs.at[0], PAD, cols)
     if base:
         shift_into(uc.at[0], us.at[0], PAD, cols)
@@ -148,25 +196,17 @@
     if base:
         pl.when(last)(lambda: start_edges([edges_c]))
 
-    def load_second_input():
-        load_u[1].wait()
-        place(uc.at[1], stage_u.at[1], 0, cols)
-        start_edges([edges_u[1]])
-        shift_into(uc.at[1], us.at[1], PAD, cols)
-
     def finish_edges(which):
-        edges_h[which].wait_recv()
-        edges_c[which].wait_recv()
+        wait_columns(edge_recv.at[which], 3 * width - 1 if base else 2 * width - 1)
         start = (PAD - width, PAD + cols)[which]
         shift_into(h_old, hs.at[0], start, width)
         edge = pl.ds((PAD - width + 1, PAD + cols)[which], width - 1)
         cell_old[edge] = cell_edge[edge].astype(jnp.float32)
         if base:
-            edges_u[0][which].wait_recv()
             shift_into(uc.at[0], us.at[0], start, width)
 
     def finish_second_input(which):
-        edges_u[1][which].wait_recv()
+        wait_columns(edge_recv.at[2 + which], width - 1)
         shift_into(uc.at[1], us.at[1], (PAD - EDGE + 1, PAD + cols)[which], EDGE - 1)
 
     def is_left(chunk):
@@ -190,15 +230,15 @@
                 pltpu.make_async_remote_copy(
                     src_ref=h_new.at[t, pl.ds(start, count)],
                     dst_ref=uc.at[t, pl.ds(start, count)],
-                    send_sem=next_send.at[t, CHUNKS.index(chunk), i],
-                    recv_sem=next_recv.at[t, CHUNKS.index(chunk), i],
+                    send_sem=next_send,
+                    recv_sem=next_recv.at[t, CHUNKS.index(chunk)],
                     device_id=(source + 1, sector),
                     device_id_type=MESH,
                 ),
                 start,
                 count,
             )
-            for i, start in enumerate(starts)
+            for start in starts
         ]
 
     def windows(center, shifted, starts, count):
@@ -246,8 +286,7 @@
         if t == steps - 1:
             cell_out[:, start:stop] = jnp.swapaxes(cell_new[PAD + start : PAD + stop], 0, 1)
 
-    for copy in load_w:
-        copy.wait()
+    pltpu.make_async_copy(weights.at[0], w, load_sem.at[5]).wait()
     load_b.wait()
     if not base:
         prepare(0, "mid")
@@ -257,6 +296,8 @@
             pl.when(far_or_last)(lambda: start_edges(soon))
         else:
             start_edges(soon)
+        if top:
+            pl.when(jnp.logical_and(far, jnp.logical_not(last)))(start_far_inputs)
 
     for block in BLOCKS:
         if (0, "side") in block:
@@ -267,17 +308,16 @@
             on_side("other", finish_edges)
         if (1, "side") in block and base:
             on_side("side", finish_second_input)
-        if (1, "other") in block:
-            if base:
-                on_side("other", finish_second_input)
-            else:
-                for t in range(steps):
-                    write_columns(t, 8, cols - 8)
-        if not base:
-            arrivals = [(t, *item) for t, chunk in block for item in to_next(t, chunk, layer - 1)]
-            for _, copy, _, _ in arrivals:
-                copy.wait_recv()
-            for t, _, start, count in arrivals:
+        if (1, "other") in block and base:
+            on_side("other", finish_second_input)
+        if base:
+            if block == BLOCKS[1]:
+                load_u[1].wait()
+        else:
+            arrivals = [(t, chunk, *piece) for t, chunk in block for piece in to_next(t, chunk, layer - 1)]
+            for t, chunk in block:
+                wait_columns(next_recv.at[t, CHUNKS.index(chunk)], sum(a[4] for a in arrivals if a[:2] == (t, chunk)))
+            for t, _, _, start, count in arrivals:
                 shift_into(uc.at[t], us.at[t], start, count)
         for t, chunk in block:
             compute(t, chunk)
@@ -286,51 +326,53 @@
             @pl.when(jnp.logical_not(last))
             def _():
                 greet()
-                start_edges(soon)
-
+                start_edges([edges_h])
+                start_inputs(0)
+                start_edges([edges_c])
+
+        if base and block == BLOCKS[1]:
+            place(uc.at[1], stage_u.at[1], 0, cols)
+            shift_into(uc.at[1], us.at[1], PAD, cols)
         if not top:
             for t, chunk in block:
                 for copy, _, _ in to_next(t, chunk, layer):
                     copy.start()
-        if block == BLOCKS[0]:
-            if base:
-                load_second_input()
-            else:
+        if base and block == BLOCKS[1]:
+            start_inputs(1)
+        if not base:
+            if block == BLOCKS[0]:
                 if layer == 1:
                     pl.when(jnp.logical_not(far_or_last))(lambda: start_edges(soon))
                 prepare(1, "mid")
-        if block == BLOCKS[1] and not base:
-            prepare(1, "near")
-        if block == BLOCKS[2] and not base:
-            pl.when(first)(start_edges_late)
+            if block == BLOCKS[1]:
+                prepare(1, "near")
+            if block == BLOCKS[2]:
+                pl.when(first)(start_edges_late)
 
     for t in range(steps):
-        write_columns(t, 0, 8)
-        write_columns(t, cols - 8, cols)
-    if base:
-        for t in range(steps):
-            write_columns(t, 8, cols - 8)
-
-    for edges in soon + edges_u[1:]:
-        for copy in edges:
-            copy.wait_send()
+        write_columns(t, 0, cols)
+
+    sent = 2 * (2 * width - 1)
+    inputs = 2 * EDGE - 1
+    if base:
+        pl.when(far)(lambda: wait_columns(edge_send, sent + inputs))
+        pl.when(jnp.logical_not(far))(lambda: wait_columns(edge_send, sent + 2 * inputs))
+    elif top:
+        pl.when(far)(lambda: wait_columns(edge_send, sent + inputs))
+        pl.when(jnp.logical_not(far))(lambda: wait_columns(edge_send, sent))
+    else:
+        wait_columns(edge_send, sent)
     if not top:
-        for block in BLOCKS:
-            for t, chunk in block:
-                for copy, _, _ in to_next(t, chunk, layer):
-                    copy.wait_send()
+        wait_columns(next_send, sum(piece[2] for block in BLOCKS for t, chunk in block for piece in to_next(t, chunk, layer)))
 
 
 def finish(h_ref, cell_ref, hidden_out, cell_out, sems):
-    steps, rows = h_ref.shape[:2]
-    half = rows // 2
-    copies = []
-    for start in (0, half):
-        part = pl.ds(start, half)
-        pairs = [(h_ref.at[t, part], hidden_out.at[0, t, part]) for t in range(steps)]
-        for source, target in pairs + [(cell_ref.at[part], cell_out.at[0, part])]:
-            copies.append(pltpu.make_async_copy(source, target, sems.at[len(copies)]))
-            copies[-1].start()
+    copies = [
+        pltpu.make_async_copy(h_ref, hidden_out.at[0], sems.at[0]),
+        pltpu.make_async_copy(cell_ref, cell_out.at[0], sems.at[1]),
+    ]
+    for copy in copies:
+        copy.start()
     for copy in copies:
         copy.wait()
 
@@ -361,6 +403,7 @@
                 pltpu.VMEM((rows, cols, chans), bf16),
                 pltpu.VMEM((rows, cols, chans), f32),
                 pltpu.VMEM((steps, rows, cols, chans), bf16),
+                pltpu.VMEM((steps, 8, rows, chans), bf16),
                 pltpu.VMEM((WIDTH, rows, chans), bf16),
                 pltpu.VMEM((steps, WIDTH, rows, chans), bf16),
                 pltpu.VMEM((steps, 2, WIDTH, rows, chans), bf16),
@@ -372,12 +415,11 @@
                 pltpu.VMEM((WIDTH, rows, chans), f32),
                 pltpu.VMEM((16 * rows, 4 * chans), f32),
                 pltpu.VMEM((14 * rows, 4 * chans), f32),
-                pltpu.SemaphoreType.DMA((5,)),
-                pltpu.SemaphoreType.DMA((9,)),
-                pltpu.SemaphoreType.DMA((8,)),
-                pltpu.SemaphoreType.DMA((8,)),
-                pltpu.SemaphoreType.DMA((steps, 4, 2)),
-                pltpu.SemaphoreType.DMA((steps, 4, 2)),
+                pltpu.SemaphoreType.DMA((6,)),
+                pltpu.SemaphoreType.DMA,
+                pltpu.SemaphoreType.DMA((4,)),
+                pltpu.SemaphoreType.DMA,
+                pltpu.SemaphoreType.DMA((steps, 4)),
                 pltpu.SemaphoreType.REGULAR,
             ],
             compiler_params=pltpu.CompilerParams(
@@ -395,7 +437,7 @@
             ],
             in_specs=[in_vmem] * 2,
             out_specs=[in_hbm] * 2,
-            scratch_shapes=[pltpu.SemaphoreType.DMA((2 * steps + 2,))],
+            scratch_shapes=[pltpu.SemaphoreType.DMA((2,))],
             compiler_params=pltpu.CompilerParams(vmem_limit_bytes=16 * 1024 * 1024),
             name="write_out",
         )(hidden, memory)

time: 23.2 us -> 21.8 us (0.940)
  Pallas kernels: 22.3 us -> 20.9 us
    pallas_call x1, Pallas kernels: 21.3 us -> 19.9 us  [local(): pl.pallas_call(lambda *refs: kernel(layers, sectors, *refs), out_shape=[p...]
where the time goes in v5:
time: 21.8 us; the launch traced here: 21.7 us
  Pallas kernels  20.9 us (96%)
  between operations  0.8 us (4%)
    pallas_call x1, Pallas kernels, local(): pl.pallas_call(lambda *refs: kernel(layers, sectors, *refs), out_shape=[p...  19.9 us
    pallas_call x1, Pallas kernels, local(): pl.pallas_call(finish, out_shape=[jax.ShapeDtypeStruct((1, steps, rows, c...  0.99 us

profile of v5, /device:TPU:33, one launch (start us, length us, event | category | flops | bytes accessed | tf_op | source)
XLA Modules:
  0.0 21.7 jit_solution(218006498933755856)
XLA Ops:
  0.6 19.9 %conv_lstm.1 = (bf16[2,32,32,128]{3,2,1,0:T(8,128)(2,1)S(1)}, f32[32,32,128]{2,1,0:T(8,128)S(1)}) custom-call(bf16[2,32,32,128]{3,2,1,0:T(8,128)(2,1)} %refs_0_.1, bf16[1,9,256,512]{3,2,1,0:T(8,128)(2,1)} %refs_1_.1, f32[1,512]{1,0:T(1,128)} %refs_2_.1, bf16[1,32,32,128]{3,2,1,0:T(8,128)(2,1)} %refs_3_.1, f32[1,32,32,128]{3,2,1,0:T(8,128)} %refs_4_.1), custom_call_target="tpu_custom_call" | custom-call | tf_op jit(solution)/shard_map/conv_lstm/pallas_call | solution.py:392
  20.6 1.0 %write_out.1 = (bf16[1,2,32,32,128]{4,3,2,1,0:T(8,128)(2,1)}, f32[1,32,32,128]{3,2,1,0:T(8,128)}) custom-call(bf16[2,32,32,128]{3,2,1,0:T(8,128)(2,1)S(1)} %get-tuple-element.4.h_ref, f32[32,32,128]{2,1,0:T(8,128)S(1)} %get-tuple-element.5.cell_ref), custom_call_target="tpu_custom_call" | custom-call | tf_op jit(solution)/shard_map/write_out/pallas_call | solution.py:432

commit v6 on v5

--- a/solution.py
+++ b/solution.py
@@ -9,10 +9,11 @@
 PAD = 8
 WIDTH = 48
 EDGE = 5
-BLOCKS = (
-    ((0, "mid"),), ((0, "near"),), ((1, "mid"),), ((1, "near"),), ((0, "side"),), ((1, "side"),), ((0, "other"),), ((1, "other"),),
+ORDER = (
+    (0, "mid"), (0, "near"), (0, "rim"), (1, "mid"), (1, "near"), (1, "rim"),
+    (0, "side"), (1, "side"), (0, "other"), (1, "other"),
 )
-CHUNKS = ("mid", "near", "side", "other")
+CHUNKS = ("mid", "near", "rim", "side", "other")
 
 
 def row_shifts(columns):
@@ -41,7 +42,7 @@
     layer, layers, sectors,
     frames, weights, biases, hidden_init, cell_init, h_out, cell_out,
     w, bias, stage_h, stage_c, stage_u, u_far, h_old, h_new, hs, uc, us, cell_old, cell_edge, cell_mid, cell_new,
-    partial_mid, partial_near, load_sem, edge_send, edge_recv, next_send, next_recv, late_sem,
+    partial_mid, partial_near, partial_rim, partial_side, load_sem, edge_send, edge_recv, next_send, next_recv, late_sem,
 ):
     sector = lax.axis_index("lon")
     right, left = lax.rem(sector + 1, sectors), lax.rem(sector + sectors - 1, sectors)
@@ -51,11 +52,21 @@
     far_right = jnp.logical_or(sector == sectors // 2 - 1, last)
     far_left = jnp.logical_or(sector == sectors // 2, first)
     far = jnp.logical_or(far_right, far_left)
+    slow = jnp.logical_or(sector == sectors // 2 - 1, sector == sectors // 2)
     far_or_last = jnp.logical_and(far, jnp.logical_not(first))
     flipped = lax.rem(sector, 4) == 3
     h_at = [h_old] + [h_new.at[t] for t in range(steps)]
     cell_at = [cell_old, cell_mid, cell_new]
-    partial = {"mid": partial_mid, "near": partial_near}
+    partial = {"mid": partial_mid, "near": partial_near, "rim": partial_rim, "side": partial_side, "other": partial_side}
+    at_start, after = [], {}
+    if not base:
+        at_start = [(0, "mid"), (0, "near"), (0, "rim")]
+        after = {(0, "mid"): (1, "mid"), (0, "rim"): (1, "near")}
+        if layer > 1:
+            at_start.append((0, "side"))
+        if layer == 2:
+            after[1, "mid"] = (1, "rim")
+    ahead = [*at_start, *after.values()] + ([(0, "other")] if layer == 1 else [])
 
     load_h = pltpu.make_async_copy(hidden_init.at[0], stage_h, load_sem.at[0])
     load_c = pltpu.make_async_copy(cell_init.at[0], stage_c, load_sem.at[1])
@@ -65,6 +76,7 @@
 
     barrier = pltpu.get_barrier_semaphore()
     load_h.start()
+    load_c.start()
     if base:
         load_u[0].start()
     pl.semaphore_signal(barrier, inc=1, device_id=(layer, left), device_id_type=MESH)
@@ -87,7 +99,6 @@
             for copy in load_u:
                 copy.start()
 
-    load_c.start()
     for copy in load_w:
         copy.start()
     load_b.start()
@@ -116,7 +127,7 @@
 
     width = EDGE - layer
     edges_h = edge_copies(0, h_old, width)
-    edges_c = edge_copies(0, cell_edge, width - 1)
+    edges_c = edge_copies(2, cell_edge, width - 1)
     edges_u = [edge_copies(t, uc.at[t], width - t) for t in range(steps)] if base else []
     soon = [edges_h, edges_c]
 
@@ -183,27 +194,29 @@
     place(h_old, stage_h, 0, cols)
     if base:
         pl.when(last)(lambda: start_edges([edges_h]))
-        load_u[0].wait()
-        place(uc.at[0], stage_u.at[0], 0, cols)
-        pl.when(last)(lambda: start_inputs(0))
-    shift_into(h_old, hs.at[0], PAD, cols)
-    if base:
-        shift_into(uc.at[0], us.at[0], PAD, cols)
     load_c.wait()
     place(cell_old, stage_c, 0, cols)
     for start in (PAD, PAD + cols - EDGE + 1):
         cell_edge[pl.ds(start, EDGE - 1)] = cell_old[pl.ds(start, EDGE - 1)].astype(jnp.bfloat16)
     if base:
         pl.when(last)(lambda: start_edges([edges_c]))
+        load_u[0].wait()
+        place(uc.at[0], stage_u.at[0], 0, cols)
+        pl.when(last)(lambda: start_inputs(0))
+        shift_into(uc.at[0], us.at[0], PAD, cols)
+    shift_into(h_old, hs.at[0], PAD, cols)
 
     def finish_edges(which):
-        wait_columns(edge_recv.at[which], 3 * width - 1 if base else 2 * width - 1)
+        wait_columns(edge_recv.at[which], 2 * width if base else width)
         start = (PAD - width, PAD + cols)[which]
         shift_into(h_old, hs.at[0], start, width)
+        if base:
+            shift_into(uc.at[0], us.at[0], start, width)
+
+    def finish_cells(which):
+        wait_columns(edge_recv.at[4 + which], width - 1)
         edge = pl.ds((PAD - width + 1, PAD + cols)[which], width - 1)
         cell_old[edge] = cell_edge[edge].astype(jnp.float32)
-        if base:
-            shift_into(uc.at[0], us.at[0], start, width)
 
     def finish_second_input(which):
         wait_columns(edge_recv.at[2 + which], width - 1)
@@ -218,9 +231,11 @@
 
     def spans(depth, chunk):
         if chunk == "mid":
-            return (PAD + 8 + depth,), 16 - 2 * depth
+            return (PAD + 10 + depth,), 12 - 2 * depth
         if chunk == "near":
-            return (PAD + 1 + depth, PAD + 24 - depth), 7
+            return (PAD + 5 + depth, PAD + 22 - depth), 5
+        if chunk == "rim":
+            return (PAD + 1 + depth, PAD + 27 - depth), 4
         return (jnp.where(is_left(chunk), PAD - 4 + depth, PAD + 31 - depth),), 5
 
     def to_next(t, chunk, source):
@@ -262,12 +277,14 @@
     def compute(t, chunk):
         starts, count = spans(layer + t, chunk)
         inputs = windows(uc.at[t], us.at[t], starts, count)
-        if chunk in partial and not base:
+        if (t, chunk) in ahead:
             sums = product(inputs, w[:, :chans])
             sums = sums + partial[chunk][pl.ds(0, sums.shape[0])]
         else:
             pairs = zip(inputs, windows(h_at[t], hs.at[t], starts, count))
             sums = product([part for pair in pairs for part in pair], w[...]) + bias[...]
+        if t == 0 and chunk in ("side", "other"):
+            on_side(chunk, finish_cells)
         memory = jnp.concatenate([cell_at[t][pl.ds(start, count)].reshape(-1, chans) for start in starts], axis=0)
         hidden, memory = gate_update(sums, memory)
         hidden = hidden.astype(jnp.bfloat16).reshape(len(starts), count, rows, chans)
@@ -289,8 +306,9 @@
     pltpu.make_async_copy(weights.at[0], w, load_sem.at[5]).wait()
     load_b.wait()
     if not base:
-        prepare(0, "mid")
-        prepare(0, "near")
+        for t, chunk in at_start:
+            if chunk != "side":
+                prepare(t, chunk)
         pl.when(jnp.logical_not(last))(greet)
         if layer == 1:
             pl.when(far_or_last)(lambda: start_edges(soon))
@@ -298,56 +316,60 @@
             start_edges(soon)
         if top:
             pl.when(jnp.logical_and(far, jnp.logical_not(last)))(start_far_inputs)
-
-    for block in BLOCKS:
-        if (0, "side") in block:
+        if (0, "side") in ahead:
+            on_side("side", finish_edges)
+            prepare(0, "side")
+
+    for t, chunk in ORDER:
+        if (t, chunk) == (0, "side"):
             if base:
                 pl.when(first)(start_edges_late)
-            on_side("side", finish_edges)
-        if (0, "other") in block:
+            if (0, "side") not in ahead:
+                on_side("side", finish_edges)
+        if (t, chunk) == (0, "other"):
             on_side("other", finish_edges)
-        if (1, "side") in block and base:
-            on_side("side", finish_second_input)
-        if (1, "other") in block and base:
-            on_side("other", finish_second_input)
+            if (0, "other") in ahead:
+                prepare(0, "other")
+        if base and t == 1 and chunk in ("side", "other"):
+            on_side(chunk, finish_second_input)
         if base:
-            if block == BLOCKS[1]:
+            if (t, chunk) == (0, "near"):
                 load_u[1].wait()
         else:
-            arrivals = [(t, chunk, *piece) for t, chunk in block for piece in to_next(t, chunk, layer - 1)]
-            for t, chunk in block:
-                wait_columns(next_recv.at[t, CHUNKS.index(chunk)], sum(a[4] for a in arrivals if a[:2] == (t, chunk)))
-            for t, _, _, start, count in arrivals:
+            arrivals = to_next(t, chunk, layer - 1)
+            wait_columns(next_recv.at[t, CHUNKS.index(chunk)], sum(count for _, _, count in arrivals))
+            for _, start, count in arrivals:
                 shift_into(uc.at[t], us.at[t], start, count)
-        for t, chunk in block:
-            compute(t, chunk)
-        if base and block == BLOCKS[0]:
-
-            @pl.when(jnp.logical_not(last))
-            def _():
-                greet()
-                start_edges([edges_h])
-                start_inputs(0)
-                start_edges([edges_c])
-
-        if base and block == BLOCKS[1]:
+        compute(t, chunk)
+        if base and (t, chunk) == (0, "near"):
             place(uc.at[1], stage_u.at[1], 0, cols)
             shift_into(uc.at[1], us.at[1], PAD, cols)
-        if not top:
-            for t, chunk in block:
-                for copy, _, _ in to_next(t, chunk, layer):
+        if base and chunk in ("mid", "near") and t == 0:
+            now = slow if chunk == "near" else jnp.logical_not(slow)
+
+            @pl.when(now)
+            def _():
+                pl.when(jnp.logical_not(last))(greet)
+                for copy, _, _ in to_next(0, "mid", layer):
                     copy.start()
-        if base and block == BLOCKS[1]:
+
+                @pl.when(jnp.logical_not(last))
+                def _():
+                    start_edges([edges_h])
+                    start_inputs(0)
+                    start_edges([edges_c])
+
+        if not top and not (base and (t, chunk) == (0, "mid")):
+            for copy, _, _ in to_next(t, chunk, layer):
+                copy.start()
+        if base and (t, chunk) == (0, "near"):
             start_inputs(1)
-        if not base:
-            if block == BLOCKS[0]:
-                if layer == 1:
-                    pl.when(jnp.logical_not(far_or_last))(lambda: start_edges(soon))
-                prepare(1, "mid")
-            if block == BLOCKS[1]:
-                prepare(1, "near")
-            if block == BLOCKS[2]:
-                pl.when(first)(start_edges_late)
+        if layer == 1 and (t, chunk) == (0, "mid"):
+            pl.when(jnp.logical_not(far_or_last))(lambda: start_edges(soon))
+        if (t, chunk) in after:
+            prepare(*after[t, chunk])
+        if not base and (t, chunk) == (1, "mid"):
+            pl.when(first)(start_edges_late)
 
     for t in range(steps):
         write_columns(t, 0, cols)
@@ -363,7 +385,7 @@
     else:
         wait_columns(edge_send, sent)
     if not top:
-        wait_columns(next_send, sum(piece[2] for block in BLOCKS for t, chunk in block for piece in to_next(t, chunk, layer)))
+        wait_columns(next_send, sum(piece[2] for t, chunk in ORDER for piece in to_next(t, chunk, layer)))
 
 
 def finish(h_ref, cell_ref, hidden_out, cell_out, sems):
@@ -413,13 +435,15 @@
                 pltpu.VMEM((WIDTH, rows, chans), bf16),
                 pltpu.VMEM((WIDTH, rows, chans), f32),
                 pltpu.VMEM((WIDTH, rows, chans), f32),
-                pltpu.VMEM((16 * rows, 4 * chans), f32),
-                pltpu.VMEM((14 * rows, 4 * chans), f32),
+                pltpu.VMEM((12 * rows, 4 * chans), f32),
+                pltpu.VMEM((10 * rows, 4 * chans), f32),
+                pltpu.VMEM((8 * rows, 4 * chans), f32),
+                pltpu.VMEM((5 * rows, 4 * chans), f32),
                 pltpu.SemaphoreType.DMA((6,)),
                 pltpu.SemaphoreType.DMA,
-                pltpu.SemaphoreType.DMA((4,)),
+                pltpu.SemaphoreType.DMA((6,)),
                 pltpu.SemaphoreType.DMA,
-                pltpu.SemaphoreType.DMA((steps, 4)),
+                pltpu.SemaphoreType.DMA((steps, 5)),
                 pltpu.SemaphoreType.REGULAR,
             ],
             compiler_params=pltpu.CompilerParams(

time: 21.8 us -> 21.9 us (level)
  the two profiles are of different devices: /device:TPU:33 before, /device:TPU:97 now
where the time goes in v6:
time: 21.9 us; the launch traced here: 21.8 us
  Pallas kernels  21 us (96%)
  between operations  0.8 us (4%)
    pallas_call x1, Pallas kernels, local(): pl.pallas_call(lambda *refs: kernel(layers, sectors, *refs), out_shape=[p...  20 us
    pallas_call x1, Pallas kernels, local(): pl.pallas_call(finish, out_shape=[jax.ShapeDtypeStruct((1, steps, rows, c...  0.99 us

profile of v6, /device:TPU:97, one launch (start us, length us, event | category | flops | bytes accessed | tf_op | source)
XLA Modules:
  0.0 21.8 jit_solution(13950758820958955558)
XLA Ops:
  0.6 20.0 %conv_lstm.1 = (bf16[2,32,32,128]{3,2,1,0:T(8,128)(2,1)S(1)}, f32[32,32,128]{2,1,0:T(8,128)S(1)}) custom-call(bf16[2,32,32,128]{3,2,1,0:T(8,128)(2,1)} %refs_0_.1, bf16[1,9,256,512]{3,2,1,0:T(8,128)(2,1)} %refs_1_.1, f32[1,512]{1,0:T(1,128)} %refs_2_.1, bf16[1,32,32,128]{3,2,1,0:T(8,128)(2,1)} %refs_3_.1, f32[1,32,32,128]{3,2,1,0:T(8,128)} %refs_4_.1), custom_call_target="tpu_custom_call" | custom-call | tf_op jit(solution)/shard_map/conv_lstm/pallas_call | solution.py:414
  20.6 1.0 %write_out.1 = (bf16[1,2,32,32,128]{4,3,2,1,0:T(8,128)(2,1)}, f32[1,32,32,128]{3,2,1,0:T(8,128)}) custom-call(bf16[2,32,32,128]{3,2,1,0:T(8,128)(2,1)S(1)} %get-tuple-element.4.h_ref, f32[32,32,128]{2,1,0:T(8,128)S(1)} %get-tuple-element.5.cell_ref), custom_call_target="tpu_custom_call" | custom-call | tf_op jit(solution)/shard_map/write_out/pallas_call | solution.py:456

commit v7 on v5

--- a/solution.py
+++ b/solution.py
@@ -41,7 +41,7 @@
     layer, layers, sectors,
     frames, weights, biases, hidden_init, cell_init, h_out, cell_out,
     w, bias, stage_h, stage_c, stage_u, u_far, h_old, h_new, hs, uc, us, cell_old, cell_edge, cell_mid, cell_new,
-    partial_mid, partial_near, load_sem, edge_send, edge_recv, next_send, next_recv, late_sem,
+    partial_mid, partial_near, partial_side, load_sem, edge_send, edge_recv, next_send, next_recv, late_sem,
 ):
     sector = lax.axis_index("lon")
     right, left = lax.rem(sector + 1, sectors), lax.rem(sector + sectors - 1, sectors)
@@ -55,7 +55,10 @@
     flipped = lax.rem(sector, 4) == 3
     h_at = [h_old] + [h_new.at[t] for t in range(steps)]
     cell_at = [cell_old, cell_mid, cell_new]
-    partial = {"mid": partial_mid, "near": partial_near}
+    partial = {"mid": partial_mid, "near": partial_near, "side": partial_side, "other": partial_side}
+    ahead = [] if base else [(0, "mid"), (0, "near"), (1, "near")]
+    if layer > 1:
+        ahead += [(1, "mid"), (0, "side")]
 
     load_h = pltpu.make_async_copy(hidden_init.at[0], stage_h, load_sem.at[0])
     load_c = pltpu.make_async_copy(cell_init.at[0], stage_c, load_sem.at[1])
@@ -64,15 +67,14 @@
     load_w = [pltpu.make_async_copy(weights.at[0, i], w.at[i], load_sem.at[5]) for i in range(9)]
 
     barrier = pltpu.get_barrier_semaphore()
-    load_h.start()
-    if base:
-        load_u[0].start()
-    pl.semaphore_signal(barrier, inc=1, device_id=(layer, left), device_id_type=MESH)
 
     @pl.when(jnp.logical_not(last))
     def _():
         pl.semaphore_signal(barrier, inc=1, device_id=(layer, right), device_id_type=MESH)
 
+    pl.semaphore_signal(barrier, inc=1, device_id=(layer, left), device_id_type=MESH)
+    load_h.start()
+    load_c.start()
     if not base:
         pl.semaphore_signal(barrier, inc=1, device_id=(layer - 1, sector), device_id_type=MESH)
     else:
@@ -80,19 +82,26 @@
         def _():
             pl.semaphore_signal(barrier, inc=1, device_id=(layers - 1, sectors - 1 - sector), device_id_type=MESH)
 
-    if top:
-
-        @pl.when(far)
-        def _():
-            for copy in load_u:
-                copy.start()
-
-    load_c.start()
-    for copy in load_w:
-        copy.start()
-    load_b.start()
+    def load_rest():
+        if base:
+            load_u[0].start()
+        if top:
+
+            @pl.when(far)
+            def _():
+                for copy in load_u:
+                    copy.start()
+
+        for copy in load_w:
+            copy.start()
+        load_b.start()
+        if base:
+            load_u[1].start()
+
     if base:
-        load_u[1].start()
+        pl.when(jnp.logical_not(last))(load_rest)
+    else:
+        load_rest()
 
     def wait_columns(sem, count):
         pair = hs.at[0, :, pl.ds(0, count // 2)] if count % 2 == 0 else hs.at[0, 0, pl.ds(0, count)]
@@ -116,7 +125,7 @@
 
     width = EDGE - layer
     edges_h = edge_copies(0, h_old, width)
-    edges_c = edge_copies(0, cell_edge, width - 1)
+    edges_c = edge_copies(2, cell_edge, width - 1)
     edges_u = [edge_copies(t, uc.at[t], width - t) for t in range(steps)] if base else []
     soon = [edges_h, edges_c]
 
@@ -183,27 +192,31 @@
     place(h_old, stage_h, 0, cols)
     if base:
         pl.when(last)(lambda: start_edges([edges_h]))
-        load_u[0].wait()
-        place(uc.at[0], stage_u.at[0], 0, cols)
-        pl.when(last)(lambda: start_inputs(0))
-    shift_into(h_old, hs.at[0], PAD, cols)
+    load_c.wait()
     if base:
-        shift_into(uc.at[0], us.at[0], PAD, cols)
-    load_c.wait()
+        pl.when(last)(load_rest)
     place(cell_old, stage_c, 0, cols)
     for start in (PAD, PAD + cols - EDGE + 1):
         cell_edge[pl.ds(start, EDGE - 1)] = cell_old[pl.ds(start, EDGE - 1)].astype(jnp.bfloat16)
     if base:
         pl.when(last)(lambda: start_edges([edges_c]))
+        load_u[0].wait()
+        place(uc.at[0], stage_u.at[0], 0, cols)
+        pl.when(last)(lambda: start_inputs(0))
+        shift_into(uc.at[0], us.at[0], PAD, cols)
+    shift_into(h_old, hs.at[0], PAD, cols)
 
     def finish_edges(which):
-        wait_columns(edge_recv.at[which], 3 * width - 1 if base else 2 * width - 1)
+        wait_columns(edge_recv.at[which], 2 * width if base else width)
         start = (PAD - width, PAD + cols)[which]
         shift_into(h_old, hs.at[0], start, width)
+        if base:
+            shift_into(uc.at[0], us.at[0], start, width)
+
+    def finish_cells(which):
+        wait_columns(edge_recv.at[4 + which], width - 1)
         edge = pl.ds((PAD - width + 1, PAD + cols)[which], width - 1)
         cell_old[edge] = cell_edge[edge].astype(jnp.float32)
-        if base:
-            shift_into(uc.at[0], us.at[0], start, width)
 
     def finish_second_input(which):
         wait_columns(edge_recv.at[2 + which], width - 1)
@@ -223,8 +236,11 @@
             return (PAD + 1 + depth, PAD + 24 - depth), 7
         return (jnp.where(is_left(chunk), PAD - 4 + depth, PAD + 31 - depth),), 5
 
-    def to_next(t, chunk, source):
+    def to_next(t, chunk, source, half=None):
         starts, count = spans(source + t, chunk)
+        if half is not None:
+            count //= 2
+            starts = (starts[0] + half * count,)
         return [
             (
                 pltpu.make_async_remote_copy(
@@ -259,15 +275,22 @@
         sums = product(windows(h_at[t], hs.at[t], starts, count), w[:, chans:]) + bias[...]
         partial[chunk][pl.ds(0, sums.shape[0])] = sums
 
-    def compute(t, chunk):
+    def compute(t, chunk, half=None):
         starts, count = spans(layer + t, chunk)
+        rows_of = pl.ds(0, len(starts) * count * rows)
+        if half is not None:
+            count //= 2
+            starts = (starts[0] + half * count,)
+            rows_of = pl.ds(half * count * rows, count * rows)
         inputs = windows(uc.at[t], us.at[t], starts, count)
-        if chunk in partial and not base:
+        if (t, chunk) in ahead:
             sums = product(inputs, w[:, :chans])
-            sums = sums + partial[chunk][pl.ds(0, sums.shape[0])]
+            sums = sums + partial[chunk][rows_of]
         else:
             pairs = zip(inputs, windows(h_at[t], hs.at[t], starts, count))
             sums = product([part for pair in pairs for part in pair], w[...]) + bias[...]
+        if t == 0 and chunk in ("side", "other"):
+            on_side(chunk, finish_cells)
         memory = jnp.concatenate([cell_at[t][pl.ds(start, count)].reshape(-1, chans) for start in starts], axis=0)
         hidden, memory = gate_update(sums, memory)
         hidden = hidden.astype(jnp.bfloat16).reshape(len(starts), count, rows, chans)
@@ -298,14 +321,20 @@
             start_edges(soon)
         if top:
             pl.when(jnp.logical_and(far, jnp.logical_not(last)))(start_far_inputs)
+        if (0, "side") in ahead:
+            on_side("side", finish_edges)
+            prepare(0, "side")
 
     for block in BLOCKS:
         if (0, "side") in block:
             if base:
                 pl.when(first)(start_edges_late)
-            on_side("side", finish_edges)
+            if (0, "side") not in ahead:
+                on_side("side", finish_edges)
         if (0, "other") in block:
             on_side("other", finish_edges)
+            if (0, "other") in ahead:
+                prepare(0, "other")
         if (1, "side") in block and base:
             on_side("side", finish_second_input)
         if (1, "other") in block and base:
@@ -319,38 +348,55 @@
                 wait_columns(next_recv.at[t, CHUNKS.index(chunk)], sum(a[4] for a in arrivals if a[:2] == (t, chunk)))
             for t, _, _, start, count in arrivals:
                 shift_into(uc.at[t], us.at[t], start, count)
+        halved = layer == 1 and block == BLOCKS[0]
         for t, chunk in block:
-            compute(t, chunk)
+            if halved:
+                for half in range(2):
+                    compute(t, chunk, half)
+                    to_next(t, chunk, layer, half)[0][0].start()
+            else:
+                if top and (t, chunk) == (1, "other"):
+                    write_columns(0, 0, cols)
+                    write_columns(1, 8, cols - 8)
+                compute(t, chunk)
+        if base and block == BLOCKS[0]:
+
+            pl.when(jnp.logical_not(last))(greet)
+
+        if base and block == BLOCKS[1]:
+            place(uc.at[1], stage_u.at[1], 0, cols)
+            shift_into(uc.at[1], us.at[1], PAD, cols)
+        if not top and not halved:
+            for t, chunk in block:
+                for copy, _, _ in to_next(t, chunk, layer):
+                    copy.start()
         if base and block == BLOCKS[0]:
 
             @pl.when(jnp.logical_not(last))
             def _():
-                greet()
                 start_edges([edges_h])
                 start_inputs(0)
                 start_edges([edges_c])
 
-        if base and block == BLOCKS[1]:
-            place(uc.at[1], stage_u.at[1], 0, cols)
-            shift_into(uc.at[1], us.at[1], PAD, cols)
-        if not top:
-            for t, chunk in block:
-                for copy, _, _ in to_next(t, chunk, layer):
-                    copy.start()
         if base and block == BLOCKS[1]:
             start_inputs(1)
         if not base:
             if block == BLOCKS[0]:
                 if layer == 1:
                     pl.when(jnp.logical_not(far_or_last))(lambda: start_edges(soon))
-                prepare(1, "mid")
+                if (1, "mid") in ahead:
+                    prepare(1, "mid")
             if block == BLOCKS[1]:
                 prepare(1, "near")
             if block == BLOCKS[2]:
                 pl.when(first)(start_edges_late)
 
-    for t in range(steps):
-        write_columns(t, 0, cols)
+    if top:
+        write_columns(1, 0, 8)
+        write_columns(1, cols - 8, cols)
+    else:
+        for t in range(steps):
+            write_columns(t, 0, cols)
 
     sent = 2 * (2 * width - 1)
     inputs = 2 * EDGE - 1
@@ -415,9 +461,10 @@
                 pltpu.VMEM((WIDTH, rows, chans), f32),
                 pltpu.VMEM((16 * rows, 4 * chans), f32),
                 pltpu.VMEM((14 * rows, 4 * chans), f32),
+                pltpu.VMEM((5 * rows, 4 * chans), f32),
                 pltpu.SemaphoreType.DMA((6,)),
                 pltpu.SemaphoreType.DMA,
-                pltpu.SemaphoreType.DMA((4,)),
+                pltpu.SemaphoreType.DMA((6,)),
                 pltpu.SemaphoreType.DMA,
                 pltpu.SemaphoreType.DMA((steps, 4)),
                 pltpu.SemaphoreType.REGULAR,

time: 21.8 us -> 21.7 us (level)
  no operation moved by 1% of the time
where the time goes in v7:
time: 21.7 us; the launch traced here: 21.5 us
  Pallas kernels  20.7 us (95%)
  between operations  0.8 us (4%)
    pallas_call x1, Pallas kernels, local(): pl.pallas_call(lambda *refs: kernel(layers, sectors, *refs), out_shape=[p...  19.7 us
    pallas_call x1, Pallas kernels, local(): pl.pallas_call(finish, out_shape=[jax.ShapeDtypeStruct((1, steps, rows, c...  0.99 us

profile of v7, /device:TPU:33, one launch (start us, length us, event | category | flops | bytes accessed | tf_op | source)
XLA Modules:
  0.0 21.5 jit_solution(15630476821195549781)
XLA Ops:
  0.6 19.7 %conv_lstm.1 = (bf16[2,32,32,128]{3,2,1,0:T(8,128)(2,1)S(1)}, f32[32,32,128]{2,1,0:T(8,128)S(1)}) custom-call(bf16[2,32,32,128]{3,2,1,0:T(8,128)(2,1)} %refs_0_.1, bf16[1,9,256,512]{3,2,1,0:T(8,128)(2,1)} %refs_1_.1, f32[1,512]{1,0:T(1,128)} %refs_2_.1, bf16[1,32,32,128]{3,2,1,0:T(8,128)(2,1)} %refs_3_.1, f32[1,32,32,128]{3,2,1,0:T(8,128)} %refs_4_.1), custom_call_target="tpu_custom_call" | custom-call | tf_op jit(solution)/shard_map/conv_lstm/pallas_call | solution.py:438
  20.4 1.0 %write_out.1 = (bf16[1,2,32,32,128]{4,3,2,1,0:T(8,128)(2,1)}, f32[1,32,32,128]{3,2,1,0:T(8,128)}) custom-call(bf16[2,32,32,128]{3,2,1,0:T(8,128)(2,1)S(1)} %get-tuple-element.4.h_ref, f32[32,32,128]{2,1,0:T(8,128)S(1)} %get-tuple-element.5.cell_ref), custom_call_target="tpu_custom_call" | custom-call | tf_op jit(solution)/shard_map/write_out/pallas_call | solution.py:479

commit v8 on v7

--- a/solution.py
+++ b/solution.py
@@ -59,6 +59,8 @@
     ahead = [] if base else [(0, "mid"), (0, "near"), (1, "near")]
     if layer > 1:
         ahead += [(1, "mid"), (0, "side")]
+    if layer == 1:
+        ahead.append((0, "other"))
 
     load_h = pltpu.make_async_copy(hidden_init.at[0], stage_h, load_sem.at[0])
     load_c = pltpu.make_async_copy(cell_init.at[0], stage_c, load_sem.at[1])
@@ -158,16 +160,16 @@
     def start_far_inputs():
         for copy in load_u:
             copy.wait()
-        for which, chosen, source in ((0, far_right, cols - 8), (1, far_left, 0)):
+        for which, chosen, source in ((0, far_right, cols - 16), (1, far_left, 0)):
 
             @pl.when(chosen)
             def _():
                 for t in range(steps):
-                    u_far[t] = jnp.swapaxes(stage_u[t, :, source : source + 8], 0, 1)
+                    u_far[t] = jnp.swapaxes(stage_u[t, :, source : source + 16], 0, 1)
                 for t in range(steps):
                     count = EDGE - t
                     pltpu.make_async_remote_copy(
-                        src_ref=u_far.at[t, pl.ds((8 - count, 0)[which], count)],
+                        src_ref=u_far.at[t, pl.ds((16 - count, 0)[which], count)],
                         dst_ref=uc.at[t, pl.ds((PAD - count, PAD + cols)[which], count)],
                         send_sem=edge_send,
                         recv_sem=edge_recv.at[2 * t + which],
@@ -304,10 +306,10 @@
                 hs[t + 1, 0, pl.ds(start, count)] = above
                 hs[t + 1, 1, pl.ds(start, count)] = below
 
-    def write_columns(t, start, stop):
-        h_out[t, :, start:stop] = jnp.swapaxes(h_new[t, PAD + start : PAD + stop], 0, 1)
+    def write_columns(t):
+        h_out[t] = jnp.swapaxes(h_new[t, PAD : PAD + cols], 0, 1)
         if t == steps - 1:
-            cell_out[:, start:stop] = jnp.swapaxes(cell_new[PAD + start : PAD + stop], 0, 1)
+            cell_out[...] = jnp.swapaxes(cell_new[PAD : PAD + cols], 0, 1)
 
     pltpu.make_async_copy(weights.at[0], w, load_sem.at[5]).wait()
     load_b.wait()
@@ -355,9 +357,6 @@
                     compute(t, chunk, half)
                     to_next(t, chunk, layer, half)[0][0].start()
             else:
-                if top and (t, chunk) == (1, "other"):
-                    write_columns(0, 0, cols)
-                    write_columns(1, 8, cols - 8)
                 compute(t, chunk)
         if base and block == BLOCKS[0]:
 
@@ -391,12 +390,8 @@
             if block == BLOCKS[2]:
                 pl.when(first)(start_edges_late)
 
-    if top:
-        write_columns(1, 0, 8)
-        write_columns(1, cols - 8, cols)
-    else:
-        for t in range(steps):
-            write_columns(t, 0, cols)
+    for t in range(steps):
+        write_columns(t)
 
     sent = 2 * (2 * width - 1)
     inputs = 2 * EDGE - 1
@@ -449,7 +444,7 @@
                 pltpu.VMEM((rows, cols, chans), bf16),
                 pltpu.VMEM((rows, cols, chans), f32),
                 pltpu.VMEM((steps, rows, cols, chans), bf16),
-                pltpu.VMEM((steps, 8, rows, chans), bf16),
+                pltpu.VMEM((steps, 16, rows, chans), bf16),
                 pltpu.VMEM((WIDTH, rows, chans), bf16),
                 pltpu.VMEM((steps, WIDTH, rows, chans), bf16),
                 pltpu.VMEM((steps, 2, WIDTH, rows, chans), bf16),

time: 21.7 us -> 21.6 us (level)
  no operation moved by 1% of the time
where the time goes in v8:
time: 21.6 us; the launch traced here: 21.4 us
  Pallas kernels  20.6 us (95%)
  between operations  0.8 us (4%)
    pallas_call x1, Pallas kernels, local(): pl.pallas_call(lambda *refs: kernel(layers, sectors, *refs), out_shape=[p...  19.7 us
    pallas_call x1, Pallas kernels, local(): pl.pallas_call(finish, out_shape=[jax.ShapeDtypeStruct((1, steps, rows, c...  0.99 us

profile of v8, /device:TPU:33, one launch (start us, length us, event | category | flops | bytes accessed | tf_op | source)
XLA Modules:
  0.0 21.4 jit_solution(17743291618569321352)
XLA Ops:
  0.6 19.7 %conv_lstm.1 = (bf16[2,32,32,128]{3,2,1,0:T(8,128)(2,1)S(1)}, f32[32,32,128]{2,1,0:T(8,128)S(1)}) custom-call(bf16[2,32,32,128]{3,2,1,0:T(8,128)(2,1)} %refs_0_.1, bf16[1,9,256,512]{3,2,1,0:T(8,128)(2,1)} %refs_1_.1, f32[1,512]{1,0:T(1,128)} %refs_2_.1, bf16[1,32,32,128]{3,2,1,0:T(8,128)(2,1)} %refs_3_.1, f32[1,32,32,128]{3,2,1,0:T(8,128)} %refs_4_.1), custom_call_target="tpu_custom_call" | custom-call | tf_op jit(solution)/shard_map/conv_lstm/pallas_call | solution.py:433
  20.3 1.0 %write_out.1 = (bf16[1,2,32,32,128]{4,3,2,1,0:T(8,128)(2,1)}, f32[1,32,32,128]{3,2,1,0:T(8,128)}) custom-call(bf16[2,32,32,128]{3,2,1,0:T(8,128)(2,1)S(1)} %get-tuple-element.4.h_ref, f32[32,32,128]{2,1,0:T(8,128)S(1)} %get-tuple-element.5.cell_ref), custom_call_target="tpu_custom_call" | custom-call | tf_op jit(solution)/shard_map/write_out/pallas_call | solution.py:474

commit v9 on v8

--- a/solution.py
+++ b/solution.py
@@ -59,7 +59,7 @@
     ahead = [] if base else [(0, "mid"), (0, "near"), (1, "near")]
     if layer > 1:
         ahead += [(1, "mid"), (0, "side")]
-    if layer == 1:
+    if layer in (1, 2):
         ahead.append((0, "other"))
 
     load_h = pltpu.make_async_copy(hidden_init.at[0], stage_h, load_sem.at[0])

time: 21.6 us -> 21.6 us (level)
  no operation moved by 1% of the time
where the time goes in v9:
time: 21.6 us; the launch traced here: 21.4 us
  Pallas kernels  20.6 us (95%)
  between operations  0.8 us (4%)
    pallas_call x1, Pallas kernels, local(): pl.pallas_call(lambda *refs: kernel(layers, sectors, *refs), out_shape=[p...  19.7 us
    pallas_call x1, Pallas kernels, local(): pl.pallas_call(finish, out_shape=[jax.ShapeDtypeStruct((1, steps, rows, c...  0.99 us

profile of v9, /device:TPU:33, one launch (start us, length us, event | category | flops | bytes accessed | tf_op | source)
XLA Modules:
  0.0 21.4 jit_solution(9748975785109929727)
XLA Ops:
  0.6 19.7 %conv_lstm.1 = (bf16[2,32,32,128]{3,2,1,0:T(8,128)(2,1)S(1)}, f32[32,32,128]{2,1,0:T(8,128)S(1)}) custom-call(bf16[2,32,32,128]{3,2,1,0:T(8,128)(2,1)} %refs_0_.1, bf16[1,9,256,512]{3,2,1,0:T(8,128)(2,1)} %refs_1_.1, f32[1,512]{1,0:T(1,128)} %refs_2_.1, bf16[1,32,32,128]{3,2,1,0:T(8,128)(2,1)} %refs_3_.1, f32[1,32,32,128]{3,2,1,0:T(8,128)} %refs_4_.1), custom_call_target="tpu_custom_call" | custom-call | tf_op jit(solution)/shard_map/conv_lstm/pallas_call | solution.py:433
  20.3 1.0 %write_out.1 = (bf16[1,2,32,32,128]{4,3,2,1,0:T(8,128)(2,1)}, f32[1,32,32,128]{3,2,1,0:T(8,128)}) custom-call(bf16[2,32,32,128]{3,2,1,0:T(8,128)(2,1)S(1)} %get-tuple-element.4.h_ref, f32[32,32,128]{2,1,0:T(8,128)S(1)} %get-tuple-element.5.cell_ref), custom_call_target="tpu_custom_call" | custom-call | tf_op jit(solution)/shard_map/write_out/pallas_call | solution.py:474
